TPU v7x, 512 devices: a whole 4x4x16 slice. The times are simulated.
512 devices in a mesh: sect: 2 (over y_hi), exp: 32 (over z, y_lo), dp: 8 (over x, core).
Axes of the slice: x: 4, y: 4 (y_hi: 2, y_lo: 2; y = y_hi * 2 + y_lo), z: 16, core: 2. Of those that a mesh axis runs over, the one named last changes fastest.
Arguments:
- decode_states: bfloat16 [1024, 2048], P('exp'), may hold values from -15 to 15
- norm_gain: float32 [2048], replicated, may hold values from 0.25 to 1.75
- decode_routes: int32 [4, 1024, 2], P(None, 'exp'), may hold values from 0 to 31, all different within a row; in each aligned block of 32 rows (0 to 31, 32 to 63, ..., all dimensions but the last counted through in order) at most 3 rows name the same one
- decode_gates: float32 [4, 1024, 2], P(None, 'exp'), may hold values from 0.2 to 1
- up_weight: bfloat16 [2, 32, 1536, 2048], P('sect', 'exp', 'dp'), may hold values from -5 to 5
- down_weight: bfloat16 [2, 32, 1536, 2048], P('sect', 'exp', 'dp'), may hold values from -5 to 5
- traj_inputs: bfloat16 [2, 1024, 2048], P('sect', 'exp'), may hold values from -6 to 6
- traj_cotangents: bfloat16 [2, 1024, 2048], P('sect', 'exp'), may hold values from -6 to 6
- traj_lengths: int32 [32, 2, 16], P('exp'), may hold values from 1 to 4, 32 in all within a row
- packing: int32 [32, 32], P('exp'), may hold values from 0 to 31, each once within a row
- learner_routes: int32 [4096, 2], P('exp'), may hold values from 0 to 31, all different within a row; in each aligned block of 128 rows (0 to 127, 128 to 255, ...) at most 12 rows name the same one
- learner_gates: float32 [4096, 2], P('exp'), may hold values from 0.2 to 1
Outputs:
- final_states: bfloat16 [1024, 2048], P('exp', 'sect')
- fresh_up: bfloat16 [2, 32, 1536, 2048], P('sect', 'exp', 'dp')
- fresh_down: bfloat16 [2, 32, 1536, 2048], P('sect', 'exp', 'dp')
Inputs may be any that keep to these rules, and one draw needn't show every extreme that they name: `decode_routes`: within each aligned block of 32 rows of one step (the rows of one index of exp), no expert is named more than 3 times, and that bound is met. `learner_routes`: within each aligned block of 128 rows (the slots of one learner shard), no expert is named more than 12 times, and that bound is met. `traj_lengths`: each row of 16 lengths sums to 32 and its largest is 4. `packing`: each row is a permutation of the 32 learner shards, so every holder sends exactly one trajectory to every shard.
All inputs are finite; a program needn't handle non-finite values.
Results may differ from a plain program's by a relative error of at most 0.02.
Values may be sent and summed in bfloat16 or wider, within the bound.
A program may use at most 64 MiB of HBM per device.

v0:
```python
import jax
import jax.numpy as jnp
from jax import lax
from jax.sharding import PartitionSpec as P

step_size = 3.0
norm_eps = 1e-06


def partner(array, axis, apart):
    return lax.ppermute(array, axis, [(i, i ^ 1 << apart) for i in range(lax.axis_size(axis))])


def slot_table(routes, experts, capacity):
    flat_routes = routes.reshape(-1)
    member = (flat_routes[:, None] == jnp.arange(experts, dtype=jnp.int32)[None, :]).astype(
        jnp.int32
    )
    earlier = jnp.cumsum(member, axis=0) - member
    within = jnp.sum(earlier * member, axis=1)
    target = flat_routes * capacity + within
    one_hot = (target[:, None] == jnp.arange(experts * capacity, dtype=jnp.int32)[None, :]).astype(
        jnp.float32
    )
    return one_hot.reshape(routes.shape[0], routes.shape[1], experts * capacity)


def pack_trajectories(held_rows, lengths, row_pack, capacity):
    traj_count = lengths.shape[1]
    per_half = held_rows.shape[0] // 2
    column_ids = jnp.arange(row_pack.shape[0], dtype=jnp.int32)
    starts = jnp.cumsum(lengths, axis=1) - lengths
    matches = (row_pack[None, :] == column_ids[:, None]).astype(jnp.int32)
    chosen = jnp.sum(matches * column_ids[None, :], axis=1)
    half_index = chosen // traj_count
    length_of = jnp.take(lengths.reshape(-1), chosen)
    first_row = half_index * per_half + jnp.take(starts.reshape(-1), chosen)
    offsets = jnp.arange(capacity, dtype=jnp.int32)
    in_length = offsets[None, :] < length_of[:, None]
    row_index = jnp.where(in_length, first_row[:, None] + offsets[None, :], 0).reshape(-1)
    picked = jnp.take(held_rows, row_index, axis=0)
    return jnp.where(in_length.reshape(-1)[:, None, None], picked, jnp.zeros_like(picked))


def across(block):
    return partner(block, "sect", 0)


def to_experts(payload):
    arrived = lax.all_to_all(payload, "exp", split_axis=0, concat_axis=0, tiled=True)
    return arrived


def sum_and_return(partial_out):
    summed = lax.psum(partial_out.astype(jnp.bfloat16), "dp")
    returned = lax.all_to_all(summed, "exp", split_axis=0, concat_axis=0, tiled=True)
    return returned


def expert_forward(arrived, up_slice, down_slice, hidden_total):
    inputs = arrived[:, 0, :]
    before_act = jnp.einsum(
        "sd,hd->sh", inputs, up_slice, preferred_element_type=jnp.float32
    ) * inputs.shape[1] ** (-0.5)
    activated = jax.nn.silu(before_act).astype(jnp.bfloat16)
    return jnp.einsum(
        "sh,hd->sd", activated, down_slice, preferred_element_type=jnp.float32
    ) * hidden_total ** (-0.5)


def learner_update(arrived, up_slice, down_slice, hidden_total):
    inputs = arrived[:, 0, :]
    scaled_grad = arrived[:, 1, :]
    model_scale = inputs.shape[1] ** (-0.5)
    hidden_scale = hidden_total ** (-0.5)
    before_act = (
        jnp.einsum("sd,hd->sh", inputs, up_slice, preferred_element_type=jnp.float32) * model_scale
    )
    sigmoid_val = jax.nn.sigmoid(before_act)
    activated = (before_act * sigmoid_val).astype(jnp.bfloat16)
    hidden_grad = (
        jnp.einsum("sd,hd->sh", scaled_grad, down_slice, preferred_element_type=jnp.float32)
        * hidden_scale
    )
    pre_grad = (hidden_grad * sigmoid_val * (1.0 + before_act * (1.0 - sigmoid_val))).astype(
        jnp.bfloat16
    )
    down_grad = (
        jnp.einsum("sh,sd->hd", activated, scaled_grad, preferred_element_type=jnp.float32)
        * hidden_scale
    )
    up_grad = (
        jnp.einsum("sh,sd->hd", pre_grad, inputs, preferred_element_type=jnp.float32) * model_scale
    )
    new_up = (up_slice.astype(jnp.float32) - step_size * up_grad).astype(jnp.bfloat16)
    new_down = (down_slice.astype(jnp.float32) - step_size * down_grad).astype(jnp.bfloat16)
    return jnp.stack([new_up, new_down])


def decode_step(
    states, norm_gain, routes, gate_values, up_slice, down_slice, is_rollout, hidden_total
):
    experts = lax.axis_size("exp")
    capacity = 3 * routes.shape[0] * routes.shape[1] // (2 * experts)
    normed = (
        states * lax.rsqrt(jnp.mean(states * states, axis=1, keepdims=True) + norm_eps) * norm_gain
    )
    normed = normed.astype(jnp.bfloat16)
    one_hot = slot_table(routes, experts, capacity)
    outgoing = jnp.einsum(
        "rks,rd->sd", one_hot.astype(jnp.bfloat16), normed, preferred_element_type=jnp.float32
    )
    arrived = to_experts(outgoing.astype(jnp.bfloat16)[:, None, :])
    partial_out = lax.cond(
        is_rollout,
        lambda: expert_forward(arrived, up_slice, down_slice, hidden_total),
        lambda: jnp.zeros((arrived.shape[0], arrived.shape[2]), jnp.float32),
    )
    returned = sum_and_return(partial_out)
    weighted = one_hot * gate_values[:, :, None]
    mixed = jnp.einsum(
        "rks,sd->rd", weighted, returned.astype(jnp.float32), precision=lax.Precision.HIGHEST
    )
    return states + mixed


def on_device(
    decode_states,
    norm_gain,
    decode_routes,
    decode_gates,
    up_weight,
    down_weight,
    traj_inputs,
    traj_cotangents,
    traj_lengths,
    packing,
    learner_routes,
    learner_gates,
):
    experts = lax.axis_size("exp")
    is_learner = lax.axis_index("sect") == 1
    is_rollout = jnp.logical_not(is_learner)
    up_here = up_weight[0, 0]
    down_here = down_weight[0, 0]
    hidden_total = up_here.shape[0] * lax.axis_size("dp")
    held_pair = jnp.stack([traj_inputs[0], traj_cotangents[0]], axis=1)
    crossed = across(held_pair)
    held_rows = jnp.concatenate([crossed, held_pair], axis=0)

    def run_steps(states, first_step, last_step, up_mat, down_mat):
        for step_index in range(first_step, last_step):
            states = decode_step(
                states,
                norm_gain,
                decode_routes[step_index],
                decode_gates[step_index],
                up_mat,
                down_mat,
                is_rollout,
                hidden_total,
            )
        return states

    total_steps = decode_routes.shape[0]
    half_steps = total_steps // 2
    states = decode_states.astype(jnp.float32)
    capacity_t = learner_routes.shape[0] // experts
    outgoing = pack_trajectories(held_rows, traj_lengths[0], packing[0], capacity_t)
    packed = lax.all_to_all(outgoing, "exp", split_axis=0, concat_axis=0, tiled=True)
    capacity_l = 3 * learner_routes.shape[0] * learner_routes.shape[1] // (2 * experts)
    one_hot = slot_table(learner_routes, experts, capacity_l).astype(jnp.bfloat16)
    token_part = jnp.einsum(
        "rks,rd->sd", one_hot, packed[:, 0, :], preferred_element_type=jnp.float32
    )
    scaled_rows = (learner_gates[:, :, None] * packed[:, 1, None, :].astype(jnp.float32)).astype(
        jnp.bfloat16
    )
    grad_part = jnp.einsum("rks,rkd->sd", one_hot, scaled_rows, preferred_element_type=jnp.float32)
    payload = jnp.stack([token_part, grad_part], axis=1).astype(jnp.bfloat16)
    arrived = to_experts(payload)
    fresh_pair = lax.cond(
        is_learner,
        lambda: learner_update(arrived, up_here, down_here, hidden_total),
        lambda: jnp.zeros((2,) + up_here.shape, jnp.bfloat16),
    )
    returned = across(fresh_pair)
    fresh_here = jnp.where(is_learner, fresh_pair, returned)
    states = run_steps(states, 0, half_steps, up_here, down_here)
    states = run_steps(states, half_steps, total_steps, fresh_here[0], fresh_here[1])
    half_width = states.shape[1] // 2
    own_half = states[:, :half_width].astype(jnp.bfloat16)
    other_half = states[:, half_width:].astype(jnp.bfloat16)
    delivered = across(other_half)
    final_states = jnp.where(is_learner, delivered, own_half)
    return (final_states, fresh_here[0][None, None], fresh_here[1][None, None])


def solution(mesh):
    in_specs = (
        P("exp", None),
        P(),
        P(None, "exp", None),
        P(None, "exp", None),
        P("sect", "exp", "dp", None),
        P("sect", "exp", "dp", None),
        P("sect", "exp", None),
        P("sect", "exp", None),
        P("exp", None, None),
        P("exp", None),
        P("exp", None),
        P("exp", None),
    )
    out_specs = (P("exp", "sect"), P("sect", "exp", "dp", None), P("sect", "exp", "dp", None))
    return jax.shard_map(
        on_device, mesh=mesh, in_specs=in_specs, out_specs=out_specs, check_vma=False
    )
```

profile of v0, /device:TPU:1, one launch (start us, length us, event | category | flops | bytes accessed | tf_op | source)
XLA Modules:
  0.0 824.8 jit_solution(11071036561187698457)
XLA Ops:
  17.2 17.0 %all-to-all-start = ((bf16[32,2,3072]{2,1,0:T(2,128)(2,1)}), bf16[32,2,3072]{2,1,0:T(2,128)(2,1)S(1)}, u32[]{:S(2)}, u32[]{:S(2)}) async-start(bf16[32,2,3072]{2,1,0:T(2,128)(2,1)} %reshape.297), calls=%async_computation | async-start | bytes 786432 | tf_op jit(solution)/shard_map/all_to_all | solution.py:50
  34.3 25.6 %all-to-all-done = bf16[32,2,3072]{2,1,0:T(2,128)(2,1)S(1)} async-done(((bf16[32,2,3072]{2,1,0:T(2,128)(2,1)}), bf16[32,2,3072]{2,1,0:T(2,128)(2,1)S(1)}, u32[]{:S(2)}, u32[]{:S(2)}) %all-to-all-start) | async-done | bytes 393248 | tf_op jit(solution)/shard_map/all_to_all | solution.py:50
  62.2 67.9 %all-reduce.5.cloned.1.call-done = bf16[32,3,2048]{2,1,0:T(4,128)(2,1)} async-done(((bf16[32,3,2048]{2,1,0:T(4,128)(2,1)}), bf16[32,3,2048]{2,1,0:T(4,128)(2,1)}) %all-reduce.5.cloned.1.call-update) | async-done | bytes 393232 | tf_op jit(solution)/shard_map/psum | solution.py:55
  130.0 12.7 %all-to-all-start.1 = ((bf16[32,3,2048]{2,1,0:T(4,128)(2,1)}), bf16[32,3,2048]{2,1,0:T(4,128)(2,1)S(1)}, u32[]{:S(2)}, u32[]{:S(2)}) async-start(bf16[32,3,2048]{2,1,0:T(4,128)(2,1)} %all-reduce.5.cloned.1.call-done), calls=%async_computation.1 | async-start | bytes 1048576 | tf_op jit(solution)/shard_map/all_to_all | solution.py:56
  150.4 21.4 %all-to-all-done.1 = bf16[32,3,2048]{2,1,0:T(4,128)(2,1)S(1)} async-done(((bf16[32,3,2048]{2,1,0:T(4,128)(2,1)}), bf16[32,3,2048]{2,1,0:T(4,128)(2,1)S(1)}, u32[]{:S(2)}, u32[]{:S(2)}) %all-to-all-start.1) | async-done | bytes 393248 | tf_op jit(solution)/shard_map/all_to_all | solution.py:56
  175.4 6.0 all-to-all-start.2
  187.9 17.2 %all-to-all-done.2 = bf16[32,2,3072]{2,1,0:T(2,128)(2,1)S(1)} async-done(((bf16[32,2,3072]{2,1,0:T(2,128)(2,1)}), bf16[32,2,3072]{2,1,0:T(2,128)(2,1)S(1)}, u32[]{:S(2)}, u32[]{:S(2)}) %all-to-all-start.2) | async-done | bytes 393248 | tf_op jit(solution)/shard_map/all_to_all | solution.py:50
  205.1 5.8 all-to-all-start.5
  215.8 46.9 %all-to-all-done.5 = bf16[128,2,2048]{2,1,0:T(2,128)(2,1)S(1)} async-done(((bf16[128,2,2048]{2,1,0:T(2,128)(2,1)}), bf16[128,2,2048]{2,1,0:T(2,128)(2,1)S(1)}, u32[]{:S(2)}, u32[]{:S(2)}) %all-to-all-start.5) | async-done | bytes 1048608 | tf_op jit(solution)/shard_map/all_to_all | solution.py:170
  262.7 33.0 %all-reduce.7.cloned.1.call-done = bf16[32,3,2048]{2,1,0:T(4,128)(2,1)} async-done(((bf16[32,3,2048]{2,1,0:T(4,128)(2,1)}), bf16[32,3,2048]{2,1,0:T(4,128)(2,1)}) %all-reduce.7.cloned.1.call-update) | async-done | bytes 393232 | tf_op jit(solution)/shard_map/psum | solution.py:55
  295.7 12.7 %all-to-all-start.3 = ((bf16[32,3,2048]{2,1,0:T(4,128)(2,1)}), bf16[32,3,2048]{2,1,0:T(4,128)(2,1)S(1)}, u32[]{:S(2)}, u32[]{:S(2)}) async-start(bf16[32,3,2048]{2,1,0:T(4,128)(2,1)} %all-reduce.7.cloned.1.call-done), calls=%async_computation.3 | async-start | bytes 1048576 | tf_op jit(solution)/shard_map/all_to_all | solution.py:56
  317.2 20.3 %all-to-all-done.3 = bf16[32,3,2048]{2,1,0:T(4,128)(2,1)S(1)} async-done(((bf16[32,3,2048]{2,1,0:T(4,128)(2,1)}), bf16[32,3,2048]{2,1,0:T(4,128)(2,1)S(1)}, u32[]{:S(2)}, u32[]{:S(2)}) %all-to-all-start.3) | async-done | bytes 393248 | tf_op jit(solution)/shard_map/all_to_all | solution.py:56
  338.3 6.0 all-to-all-start.6
  347.9 135.7 %all-to-all-done.6 = bf16[384,2,2048]{2,1,0:T(2,128)(2,1)S(1)} async-done(((bf16[384,2,2048]{2,1,0:T(2,128)(2,1)}), bf16[384,2,2048]{2,1,0:T(2,128)(2,1)S(1)}, u32[]{:S(2)}, u32[]{:S(2)}) %all-to-all-start.6) | async-done | bytes 3145760 | tf_op jit(solution)/shard_map/all_to_all | solution.py:50
  484.0 13.9 %collective-permute-start.1 = (bf16[2,192,2048]{2,1,0:T(8,128)(2,1)S(1)}, bf16[2,192,2048]{2,1,0:T(8,128)(2,1)S(1)}, u32[]{:S(2)}, u32[]{:S(2)}) collective-permute-start(bf16[2,192,2048]{2,1,0:T(8,128)(2,1)S(1)} %get-tuple-element.162), channel_id=1, source_target_pairs={{0,256},{256,0},{1,257},{257,1},{2,258},{258,2},{3,259},{259,3},{4... | collective-permute-start | bytes 4718600 | tf_op jit(solution)/shard_map/ppermute | solution.py:11
  503.5 8.9 %all-to-all-start.4 = ((bf16[32,2,3072]{2,1,0:T(2,128)(2,1)}), bf16[32,2,3072]{2,1,0:T(2,128)(2,1)}, u32[]{:S(2)}, u32[]{:S(2)}) async-start(bf16[32,2,3072]{2,1,0:T(2,128)(2,1)} %reshape.301), calls=%async_computation.4 | async-start | bytes 786432 | tf_op jit(solution)/shard_map/all_to_all | solution.py:50
  512.5 24.9 %all-to-all-done.4 = bf16[32,2,3072]{2,1,0:T(2,128)(2,1)} async-done(((bf16[32,2,3072]{2,1,0:T(2,128)(2,1)}), bf16[32,2,3072]{2,1,0:T(2,128)(2,1)}, u32[]{:S(2)}, u32[]{:S(2)}) %all-to-all-start.4) | async-done | bytes 393248 | tf_op jit(solution)/shard_map/all_to_all | solution.py:50
  545.6 73.4 %all-reduce.9.cloned.1.call-done = bf16[32,3,2048]{2,1,0:T(4,128)(2,1)} async-done(((bf16[32,3,2048]{2,1,0:T(4,128)(2,1)}), bf16[32,3,2048]{2,1,0:T(4,128)(2,1)}) %all-reduce.9.cloned.1.call-update) | async-done | bytes 393232 | tf_op jit(solution)/shard_map/psum | solution.py:55
  619.0 12.7 %all-to-all-start.7 = ((bf16[32,3,2048]{2,1,0:T(4,128)(2,1)}), bf16[32,3,2048]{2,1,0:T(4,128)(2,1)S(1)}, u32[]{:S(2)}, u32[]{:S(2)}) async-start(bf16[32,3,2048]{2,1,0:T(4,128)(2,1)} %all-reduce.9.cloned.1.call-done), calls=%async_computation.7 | async-start | bytes 1048576 | tf_op jit(solution)/shard_map/all_to_all | solution.py:56
  631.7 29.0 %all-to-all-done.7 = bf16[32,3,2048]{2,1,0:T(4,128)(2,1)S(1)} async-done(((bf16[32,3,2048]{2,1,0:T(4,128)(2,1)}), bf16[32,3,2048]{2,1,0:T(4,128)(2,1)S(1)}, u32[]{:S(2)}, u32[]{:S(2)}) %all-to-all-start.7) | async-done | bytes 393248 | tf_op jit(solution)/shard_map/all_to_all | solution.py:56
  663.7 6.0 all-to-all-start.8
  669.8 23.5 %all-to-all-done.8 = bf16[32,2,3072]{2,1,0:T(2,128)(2,1)S(1)} async-done(((bf16[32,2,3072]{2,1,0:T(2,128)(2,1)}), bf16[32,2,3072]{2,1,0:T(2,128)(2,1)S(1)}, u32[]{:S(2)}, u32[]{:S(2)}) %all-to-all-start.8) | async-done | bytes 393248 | tf_op jit(solution)/shard_map/all_to_all | solution.py:50
  697.3 71.4 %all-reduce.11.cloned.1.call-done = bf16[32,3,2048]{2,1,0:T(4,128)(2,1)} async-done(((bf16[32,3,2048]{2,1,0:T(4,128)(2,1)}), bf16[32,3,2048]{2,1,0:T(4,128)(2,1)}) %all-reduce.11.cloned.1.call-update) | async-done | bytes 393232 | tf_op jit(solution)/shard_map/psum | solution.py:55
  768.7 41.7 %all_to_all.78 = bf16[32,3,2048]{2,1,0:T(4,128)(2,1)S(1)} all-to-all(bf16[32,3,2048]{2,1,0:T(4,128)(2,1)} %all-reduce.11.cloned.1.call-done), channel_id=1, replica_groups=mesh['sect'=2,'exp'=32,'dp'=8] {'exp'}, dimensions={0} | all-to-all | bytes 786432 | tf_op jit(solution)/shard_map/all_to_all | solution.py:56
  (163 shorter events, 83.6 us)
Async XLA Ops:
  16.2 44.1 %copy-start.12 = (bf16[1,1,192,2048]{3,2,1,0:T(8,128)(2,1)S(1)}, bf16[1,1,192,2048]{3,2,1,0:T(8,128)(2,1)}, u32[]{:S(2)}) copy-start(bf16[1,1,192,2048]{3,2,1,0:T(8,128)(2,1)} %param.28) | copy-start | bytes 2359300
  16.2 44.1 %copy-start.14 = (bf16[1,1,192,2048]{3,2,1,0:T(8,128)(2,1)S(1)}, bf16[1,1,192,2048]{3,2,1,0:T(8,128)(2,1)}, u32[]{:S(2)}) copy-start(bf16[1,1,192,2048]{3,2,1,0:T(8,128)(2,1)} %param.29) | copy-start | bytes 2359300
  17.2 42.7 %all-to-all-start = ((bf16[32,2,3072]{2,1,0:T(2,128)(2,1)}), bf16[32,2,3072]{2,1,0:T(2,128)(2,1)S(1)}, u32[]{:S(2)}, u32[]{:S(2)}) async-start(bf16[32,2,3072]{2,1,0:T(2,128)(2,1)} %reshape.297), calls=%async_computation | async-start | bytes 786432 | tf_op jit(solution)/shard_map/all_to_all | solution.py:50
  34.3 95.8 %all-reduce.5.cloned.1.call-start = ((), (), s32[]{:S(2)}) async-start(), calls=%async_computation.10 | async-start | bytes 1048576 | tf_op jit(solution)/shard_map/psum | solution.py:55
  61.1 81.6 %copy-start.7 = (bf16[1,32,2048]{2,1,0:T(8,128)(2,1)S(1)}, bf16[1,32,2048]{2,1,0:T(8,128)(2,1)}, u32[]{:S(2)}) copy-start(bf16[1,32,2048]{2,1,0:T(8,128)(2,1)} %param.30) | copy-start | bytes 393220
  61.1 81.8 %copy-start.8 = (bf16[1,32,2048]{2,1,0:T(8,128)(2,1)S(1)}, bf16[1,32,2048]{2,1,0:T(8,128)(2,1)}, u32[]{:S(2)}) copy-start(bf16[1,32,2048]{2,1,0:T(8,128)(2,1)} %param.31) | copy-start | bytes 393220
  62.2 86.0 %copy-start.11 = (s32[1,2,16]{2,1,0:T(2,128)S(1)}, s32[1,2,16]{2,1,0:T(2,128)}, u32[]{:S(2)}) copy-start(s32[1,2,16]{2,1,0:T(2,128)} %param.32) | copy-start | bytes 388
  62.2 86.4 %copy-start.15 = (s32[1,32]{1,0:T(1,128)S(1)}, s32[1,32]{1,0:T(1,128)}, u32[]{:S(2)}) copy-start(s32[1,32]{1,0:T(1,128)} %param.33) | copy-start | bytes 388
  130.0 41.7 %all-to-all-start.1 = ((bf16[32,3,2048]{2,1,0:T(4,128)(2,1)}), bf16[32,3,2048]{2,1,0:T(4,128)(2,1)S(1)}, u32[]{:S(2)}, u32[]{:S(2)}) async-start(bf16[32,3,2048]{2,1,0:T(4,128)(2,1)} %all-reduce.5.cloned.1.call-done), calls=%async_computation.1 | async-start | bytes 1048576 | tf_op jit(solution)/shard_map/all_to_all | solution.py:56
  142.9 29.2 %copy-start.4 = (bf16[32,2048]{1,0:T(8,128)(2,1)S(1)}, bf16[32,2048]{1,0:T(8,128)(2,1)}, u32[]{:S(2)}) copy-start(bf16[32,2048]{1,0:T(8,128)(2,1)} %param.24) | copy-start | bytes 393220
  143.8 29.4 %copy-start.6 = (f32[2048]{0:T(1024)S(1)}, f32[2048]{0:T(1024)}, u32[]{:S(2)}) copy-start(f32[2048]{0:T(1024)} %param.25) | copy-start | bytes 24580
  143.8 38.0 %collective-permute-start = (bf16[32,2,2048]{2,1,0:T(2,128)(2,1)S(1)}, bf16[32,2,2048]{2,1,0:T(2,128)(2,1)S(1)}, u32[]{:S(2)}, u32[]{:S(2)}) collective-permute-start(bf16[32,2,2048]{2,1,0:T(2,128)(2,1)S(1)} %pad_maximum_fusion.2), channel_id=1, source_target_pairs={{0,256},{256,0},{1,257},{257,1},{2,258},{258,2},{3,259},{259,3},{4... | collective-permute-start | bytes 786440 | tf_op jit(solution)/shard_map/ppermute | solution.py:11
  175.4 29.6 %all-to-all-start.2 = ((bf16[32,2,3072]{2,1,0:T(2,128)(2,1)}), bf16[32,2,3072]{2,1,0:T(2,128)(2,1)S(1)}, u32[]{:S(2)}, u32[]{:S(2)}) async-start(bf16[32,2,3072]{2,1,0:T(2,128)(2,1)} %reshape.299), calls=%async_computation.2 | async-start | bytes 786432 | tf_op jit(solution)/shard_map/all_to_all | solution.py:50
  205.1 57.6 %all-to-all-start.5 = ((bf16[128,2,2048]{2,1,0:T(2,128)(2,1)}), bf16[128,2,2048]{2,1,0:T(2,128)(2,1)S(1)}, u32[]{:S(2)}, u32[]{:S(2)}) async-start(bf16[128,2,2048]{2,1,0:T(2,128)(2,1)} %broadcast_select_fusion.1), calls=%async_computation.5 | async-start | bytes 2097152 | tf_op jit(solution)/shard_map/all_to_all | solution.py:170
  210.9 84.9 %all-reduce.7.cloned.1.call-start = ((), (), s32[]{:S(2)}) async-start(), calls=%async_computation.11 | async-start | bytes 1048576 | tf_op jit(solution)/shard_map/psum | solution.py:55
  295.7 41.7 %all-to-all-start.3 = ((bf16[32,3,2048]{2,1,0:T(4,128)(2,1)}), bf16[32,3,2048]{2,1,0:T(4,128)(2,1)S(1)}, u32[]{:S(2)}, u32[]{:S(2)}) async-start(bf16[32,3,2048]{2,1,0:T(4,128)(2,1)} %all-reduce.7.cloned.1.call-done), calls=%async_computation.3 | async-start | bytes 1048576 | tf_op jit(solution)/shard_map/all_to_all | solution.py:56
  338.3 145.3 %all-to-all-start.6 = ((bf16[384,2,2048]{2,1,0:T(2,128)(2,1)}), bf16[384,2,2048]{2,1,0:T(2,128)(2,1)S(1)}, u32[]{:S(2)}, u32[]{:S(2)}) async-start(bf16[384,2,2048]{2,1,0:T(2,128)(2,1)} %copy.159), calls=%async_computation.6 | async-start | bytes 6291456 | tf_op jit(solution)/shard_map/all_to_all | solution.py:50
  484.0 56.9 %collective-permute-start.1 = (bf16[2,192,2048]{2,1,0:T(8,128)(2,1)S(1)}, bf16[2,192,2048]{2,1,0:T(8,128)(2,1)S(1)}, u32[]{:S(2)}, u32[]{:S(2)}) collective-permute-start(bf16[2,192,2048]{2,1,0:T(8,128)(2,1)S(1)} %get-tuple-element.162), channel_id=1, source_target_pairs={{0,256},{256,0},{1,257},{257,1},{2,258},{258,2},{3,259},{259,3},{4... | collective-permute-start | bytes 4718600 | tf_op jit(solution)/shard_map/ppermute | solution.py:11
  503.5 33.9 %all-to-all-start.4 = ((bf16[32,2,3072]{2,1,0:T(2,128)(2,1)}), bf16[32,2,3072]{2,1,0:T(2,128)(2,1)}, u32[]{:S(2)}, u32[]{:S(2)}) async-start(bf16[32,2,3072]{2,1,0:T(2,128)(2,1)} %reshape.301), calls=%async_computation.4 | async-start | bytes 786432 | tf_op jit(solution)/shard_map/all_to_all | solution.py:50
  512.5 106.5 %all-reduce.9.cloned.1.call-start = ((), (), s32[]{:S(2)}) async-start(), calls=%async_computation.12 | async-start | bytes 1048576 | tf_op jit(solution)/shard_map/psum | solution.py:55
  619.0 41.7 %all-to-all-start.7 = ((bf16[32,3,2048]{2,1,0:T(4,128)(2,1)}), bf16[32,3,2048]{2,1,0:T(4,128)(2,1)S(1)}, u32[]{:S(2)}, u32[]{:S(2)}) async-start(bf16[32,3,2048]{2,1,0:T(4,128)(2,1)} %all-reduce.9.cloned.1.call-done), calls=%async_computation.7 | async-start | bytes 1048576 | tf_op jit(solution)/shard_map/all_to_all | solution.py:56
  663.7 29.6 %all-to-all-start.8 = ((bf16[32,2,3072]{2,1,0:T(2,128)(2,1)}), bf16[32,2,3072]{2,1,0:T(2,128)(2,1)S(1)}, u32[]{:S(2)}, u32[]{:S(2)}) async-start(bf16[32,2,3072]{2,1,0:T(2,128)(2,1)} %reshape.303), calls=%async_computation.8 | async-start | bytes 786432 | tf_op jit(solution)/shard_map/all_to_all | solution.py:50
  669.7 99.0 %all-reduce.11.cloned.1.call-start = ((), (), s32[]{:S(2)}) async-start(), calls=%async_computation.13 | async-start | bytes 1048576 | tf_op jit(solution)/shard_map/psum | solution.py:55
  811.1 6.5 collective-permute-start.2
  (4 other events, 25.3 us)
Sparse Core Ops, SparseCore 0:
  62.3 67.6 all-reduce.4
  214.9 80.7 all-reduce.6
  545.7 73.2 all-reduce.8
  697.5 71.2 all-reduce.10
where the time goes:
time: 831 us; the launch traced here: 825 us
  waiting for transfers between devices  592 us (71%)
  starting transfers between devices  111 us (13%)
  blocking collectives  41.7 us (5%)
  local copies, waits for them, and re-layouts  35.2 us (4%)
  other arithmetic  16.6 us (2%)
  between operations  14.4 us (2%)
  matrix products  13.5 us (2%)
    psum x4, waiting for transfers between devices, sum_and_return(): summed = lax.psum(partial_out.astype(jnp.bfloat16), 'dp')  246 us
    all_to_all x5, waiting for transfers between devices, to_experts(): lax.all_to_all(payload, 'exp', split_axis=0, concat_axis=0, tiled=True)  227 us
    all_to_all x3, waiting for transfers between devices, sum_and_return(): lax.all_to_all(summed, 'exp', split_axis=0, concat_axis=0, tiled=True)  70.7 us
    all_to_all x1, waiting for transfers between devices, on_device(): lax.all_to_all(outgoing, 'exp', split_axis=0, concat_axis=0, tiled=True)  46.9 us
    all_to_all x5, starting transfers between devices, to_experts(): lax.all_to_all(payload, 'exp', split_axis=0, concat_axis=0, tiled=True)  44.1 us
    all_to_all x1, blocking collectives, sum_and_return(): lax.all_to_all(summed, 'exp', split_axis=0, concat_axis=0, tiled=True)  41.7 us
    all_to_all x3, starting transfers between devices, sum_and_return(): lax.all_to_all(summed, 'exp', split_axis=0, concat_axis=0, tiled=True)  38 us
    ppermute x3, starting transfers between devices, partner(): lax.ppermute(array, axis, [(i, i ^ 1 << apart) for i in range(lax.axis_si...  22.6 us
  transfers between devices with their start and end apart: 16, of which 14 were waited for; matrix products, arithmetic and copies ran while one was open for 4% of the time, Pallas kernels for 0%

commit v1 on v0

v1 whole, which is shorter than its diff:
```python
import functools

import jax
import jax.numpy as jnp
import ml_dtypes
import numpy as np
from jax import lax
from jax.experimental import pallas as pl
from jax.experimental.pallas import tpu as pltpu
from jax.sharding import PartitionSpec as P

MESH = pl.DeviceIdType.MESH
step_size = 3.0
norm_eps = 1e-06
f32 = jnp.float32
bf16 = jnp.bfloat16
LANES = 128
GROUPS = 4


def dot(a, b):
    return lax.dot_general(a, b, (((1,), (0,)), ((), ())), preferred_element_type=f32)


def dot_nt(a, b):
    return lax.dot_general(a, b, (((1,), (1,)), ((), ())), preferred_element_type=f32)


def dot_tn(a, b):
    return lax.dot_general(a, b, (((0,), (0,)), ((), ())), preferred_element_type=f32)


def iota(shape, dim):
    return lax.broadcasted_iota(jnp.int32, shape, dim).astype(f32)


def to_row(col):
    n = col.shape[0]
    eye = iota((n, n), 0) == iota((n, n), 1)
    return jnp.sum(jnp.where(eye, col, 0.0), axis=0, keepdims=True)


def to_col(row):
    n = row.shape[1]
    eye = iota((n, n), 0) == iota((n, n), 1)
    return jnp.sum(jnp.where(eye, row, 0.0), axis=1, keepdims=True)


def ranks(first, second):
    n = first.shape[0]
    first_row, second_row = to_row(first), to_row(second)
    before = iota((n, n), 1) < iota((n, n), 0)
    out = []
    for mine in (first, second):
        same = ((first_row == mine) | (second_row == mine)) & before
        out.append(jnp.sum(jnp.where(same, 1.0, 0.0), axis=1, keepdims=True))
    return out


def permutations(experts, cap_d, cap_l):
    slots = experts * cap_d
    take_d = np.zeros((2 * slots, experts * 8), np.float32)
    for c in range(2):
        for k in range(experts):
            for s in range(cap_d):
                take_d[c * slots + k * cap_d + s, k * 8 + c * 4 + s] = 1
    give_d = np.stack([take_d[:slots].T, take_d[slots:].T])
    per = experts // GROUPS
    take_l = np.zeros((per * cap_l * 2, per * cap_l * 2), np.float32)
    for c in range(2):
        for k in range(per):
            for s in range(cap_l):
                take_l[c * per * cap_l + k * cap_l + s, k * 2 * cap_l + c * cap_l + s] = 1
    return [m.astype(ml_dtypes.bfloat16) for m in (take_d, give_d, take_l)]


def kernel(
    experts, shards, cap_d, cap_l,
    rows_ref, gain_ref, routes_ref, gates_ref, up_ref, down_ref, in_ref, cot_ref, len_ref, pack_ref,
    lroutes_ref, lgates_ref, take_d_ref, give_d_ref, take_l_ref,
    final_ref, fresh_up_ref, fresh_down_ref,
    d1_out, d1_in, xg, d3_out, d3_in, d4_out, d4_in, states_ref, trow_ref, tcol_ref,
    held, out2, recv2, out3, recv3, xg4, act_ref, pre_ref, fin_src,
    dec_sem, l1_sem, l2_sem, st_sem, fin_sem, fresh_sem, l3_send, l3_recv, l4_send, l4_recv,
):
    sect, me, dp = lax.axis_index("sect"), lax.axis_index("exp"), lax.axis_index("dp")
    ring, core = lax.div(dp, 2), lax.rem(dp, 2)
    other = 1 - sect
    width = rows_ref.shape[1]
    part = width // shards
    hidden = up_ref.shape[0]
    model_scale = width ** (-0.5)
    hidden_scale = (hidden * shards) ** (-0.5)
    dec_rows = rows_ref.shape[0]
    slots = experts * cap_d
    per = experts // GROUPS
    group_slots = per * cap_l
    col0 = pl.multiple_of(dp * part, part)

    def rcopy(src, dst, send, recv, device):
        return pltpu.make_async_remote_copy(
            src_ref=src, dst_ref=dst, send_sem=send, recv_sem=recv, device_id=device, device_id_type=MESH
        )

    def wait_sent(ref, sem):
        rcopy(ref, ref, sem, sem, (sect, me, dp)).wait_send()

    def wait_here(ref, sem):
        rcopy(ref, ref, sem, sem, (sect, me, dp)).wait_recv()

    def others(fn):
        def one(i, carry):
            half = lax.div(i + 1, 2)
            fn(jnp.where(lax.rem(i, 2) == 1, half, experts - half))
            return carry

        lax.fori_loop(1, experts, one, 0)

    barrier = pltpu.get_barrier_semaphore()

    def greet_exp(k):
        pl.semaphore_signal(barrier, inc=1, device_id=(sect, lax.rem(me + k, experts), dp), device_id_type=MESH)

    others(greet_exp)
    for q in range(1, shards):
        pl.semaphore_signal(barrier, inc=1, device_id=(sect, me, lax.rem(dp + q, shards)), device_id_type=MESH)
    for q in range(shards):
        pl.semaphore_signal(barrier, inc=1, device_id=(other, me, lax.rem(dp + q, shards)), device_id_type=MESH)
    pl.semaphore_wait(barrier, experts - 1 + shards - 1 + shards)

    @pl.when(sect == 0)
    def _():
        rcopy(in_ref.at[:, pl.ds(col0, part)], held.at[0], l1_sem.at[0], l1_sem.at[1], (other, me, dp)).start()
        rcopy(cot_ref.at[:, pl.ds(col0, part)], held.at[1], l1_sem.at[0], l1_sem.at[1], (other, me, dp)).start()

    def tables(i, t):
        routes = routes_ref[t].astype(f32)
        first, second = routes[:, 0:1], routes[:, 1:2]
        within = ranks(first, second)
        for k, mine in enumerate((first, second)):
            target = mine * 8.0 + within[k]
            both = jnp.concatenate([target, target + 4.0], axis=0)
            tcol_ref[i, k] = both
            trow_ref[i, k] = to_row(both)

    def decode_step(i, t, up, down):
        gain0, gain1 = gain_ref[pl.ds(2 * dp, 1), :], gain_ref[pl.ds(2 * dp + 1, 1), :]
        gains = jnp.concatenate(
            [jnp.broadcast_to(gain0, (dec_rows, LANES)), jnp.broadcast_to(gain1, (dec_rows, LANES))], axis=0
        )
        y = (states_ref[...] * gains).astype(bf16)
        row_ids = iota((experts * 8, 2 * dec_rows), 0)
        pick = (row_ids == trow_ref[i, 0]) | (row_ids == trow_ref[i, 1])
        pick = jnp.where(pick, 1.0, 0.0).astype(bf16)
        d1_out[i] = dot(pick, y).astype(bf16).reshape(experts, 8, LANES)
        d1_in[i, me] = d1_out[i, me]

        def send1(k):
            to = lax.rem(me + k, experts)
            rcopy(d1_out.at[i, to], d1_in.at[i, me], dec_sem.at[0, i, 0], dec_sem.at[0, i, 1], (sect, to, dp)).start()

        others(send1)
        wait_here(d1_in.at[i, pl.ds(0, experts - 1)], dec_sem.at[0, i, 1])
        block = dot(take_d_ref[...], d1_in[i].reshape(experts * 8, LANES)).astype(bf16)
        xg[i, dp] = jnp.concatenate([block[:slots], block[slots:]], axis=1)

        def send2(q, carry):
            to = lax.rem(dp + q, shards)
            rcopy(xg.at[i, dp], xg.at[i, dp], dec_sem.at[1, i, 0], dec_sem.at[1, i, 1], (sect, me, to)).start()
            return carry

        lax.fori_loop(1, shards, send2, 0)
        wait_here(xg.at[i, pl.ds(0, shards - 1)], dec_sem.at[1, i, 1])
        before_act = jnp.zeros((slots, hidden), f32)
        squares = jnp.zeros((slots, part), f32)
        for q in range(shards):
            piece = xg[i, q]
            before_act += dot_nt(piece, up[:, q * part : (q + 1) * part])
            gain = jnp.concatenate([gain_ref[2 * q : 2 * q + 1], gain_ref[2 * q + 1 : 2 * q + 2]], axis=1)
            wide = piece.astype(f32) / gain
            squares += wide * wide
        mean = jnp.sum(squares, axis=1, keepdims=True) * (1.0 / width)
        before_act = before_act * (lax.rsqrt(mean + norm_eps) * model_scale)
        act = (before_act / (1.0 + jnp.exp(-before_act))).astype(bf16)
        for q in range(shards):
            d3_out[i, q] = (dot(act, down[:, q * part : (q + 1) * part]) * hidden_scale).astype(bf16)
        d3_in[i, dp] = d3_out[i, dp]

        def send3(q, carry):
            to = lax.rem(dp + q, shards)
            rcopy(d3_out.at[i, to], d3_in.at[i, dp], dec_sem.at[2, i, 0], dec_sem.at[2, i, 1], (sect, me, to)).start()
            return carry

        lax.fori_loop(1, shards, send3, 0)
        wait_here(d3_in.at[i, pl.ds(0, shards - 1)], dec_sem.at[2, i, 1])
        total = d3_in[i, 0].astype(f32)
        for q in range(1, shards):
            total += d3_in[i, q].astype(f32)
        total = total.astype(bf16)
        back = dot(give_d_ref[0], total[:, :LANES]) + dot(give_d_ref[1], total[:, LANES:])
        d4_out[i] = back.astype(bf16).reshape(experts, 8, LANES)
        d4_in[i, me] = d4_out[i, me]

        def send4(k):
            to = lax.rem(me + k, experts)
            rcopy(d4_out.at[i, to], d4_in.at[i, me], dec_sem.at[3, i, 0], dec_sem.at[3, i, 1], (sect, to, dp)).start()

        others(send4)
        lane_ids = iota((2 * dec_rows, experts * 8), 1)
        gate = gates_ref[t]
        gate = jnp.concatenate([gate, gate], axis=0)
        mix = jnp.where(lane_ids == tcol_ref[i, 0], gate[:, 0:1], 0.0)
        mix += jnp.where(lane_ids == tcol_ref[i, 1], gate[:, 1:2], 0.0)
        high = mix.astype(bf16)
        rest = mix - high.astype(f32)
        middle = rest.astype(bf16)
        low = (rest - middle.astype(f32)).astype(bf16)
        wait_here(d4_in.at[i, pl.ds(0, experts - 1)], dec_sem.at[3, i, 1])
        returned = d4_in[i].reshape(experts * 8, LANES)
        states_ref[...] += dot(high, returned) + (dot(middle, returned) + dot(low, returned))

    def decode_sent(i):
        wait_sent(d1_out.at[i, pl.ds(0, experts - 1)], dec_sem.at[0, i, 0])
        wait_sent(xg.at[i, pl.ds(0, shards - 1)], dec_sem.at[1, i, 0])
        wait_sent(d3_out.at[i, pl.ds(0, shards - 1)], dec_sem.at[2, i, 0])
        wait_sent(d4_out.at[i, pl.ds(0, experts - 1)], dec_sem.at[3, i, 0])

    @pl.when(sect == 0)
    def _():
        for i in range(2):
            tables(i, i)
        states_ref[...] = jnp.concatenate(
            [
                rows_ref[:, pl.ds(col0, LANES)].astype(f32),
                rows_ref[:, pl.ds(pl.multiple_of(col0 + LANES, LANES), LANES)].astype(f32),
            ],
            axis=0,
        )
        for i in range(2):
            decode_step(i, i, up_ref, down_ref)
        move = rcopy(states_ref, states_ref, st_sem.at[0], st_sem.at[1], (other, me, dp))
        move.start()
        move.wait_send()
        wait_sent(held, l1_sem.at[0])
        for i in range(2):
            decode_sent(i)
        wait_here(fresh_up_ref, fresh_sem.at[0, 1])
        wait_here(fresh_down_ref, fresh_sem.at[1, 1])
        wait_here(final_ref, fin_sem.at[1])

    @pl.when(sect == 1)
    def _():
        lengths = len_ref[...].astype(f32)
        count = lengths.shape[1]
        length = jnp.concatenate([to_col(lengths[0:1]), to_col(lengths[1:2])], axis=0)
        both = 2 * count
        a, b = iota((both, both), 0), iota((both, both), 1)
        same_half = (a < count) == (b < count)
        start_row = jnp.sum(jnp.where(same_half & (a < b), length, 0.0), axis=0, keepdims=True)
        length_row = to_row(length)
        half_rows = held.shape[1]
        r, t = iota((2 * half_rows, both), 0), iota((2 * half_rows, both), 1)
        second = r >= half_rows
        row_in = r - jnp.where(second, float(half_rows), 0.0)
        offset = row_in - start_row
        inside = (second == (t >= count)) & (offset >= 0.0) & (offset < length_row)
        shard = pack_ref[...].astype(f32)
        target2 = jnp.sum(jnp.where(inside, shard * 8.0 + offset, 0.0), axis=1, keepdims=True)
        target2 = to_row(jnp.concatenate([target2, target2 + 4.0], axis=0))
        row_ids = iota((experts * 8, 4 * half_rows), 0)
        pack = jnp.where(row_ids == target2, 1.0, 0.0).astype(bf16)
        wait_here(held, l1_sem.at[1])
        for j, own_ref in enumerate((in_ref, cot_ref)):
            far = held[j]
            own = own_ref[:, pl.ds(col0, part)]
            stacked = jnp.concatenate([far[:, :LANES], own[:, :LANES], far[:, LANES:], own[:, LANES:]], axis=0)
            out2[j] = dot(pack, stacked).astype(bf16).reshape(experts, 8, LANES)
            recv2[j, me] = out2[j, me]

        def send_l2(k):
            to = lax.rem(me + k, experts)
            rcopy(out2.at[:, to], recv2.at[:, me], l2_sem.at[0], l2_sem.at[1], (sect, to, dp)).start()

        others(send_l2)

        lroutes = lroutes_ref[...].astype(f32)
        first, second = lroutes[:, 0:1], lroutes[:, 1:2]
        within = ranks(first, second)
        lgates = lgates_ref[...]

        def by_half(col, step):
            n = col.shape[0]
            row = jnp.zeros((1, 2 * n), f32)
            r, l = iota((n, 2 * n), 0), iota((n, 2 * n), 1)
            source = jnp.floor(r * 0.25)
            place = source * 4.0 + r
            row += jnp.sum(jnp.where(l == place, col, 0.0), axis=0, keepdims=True)
            row += jnp.sum(jnp.where(l == place + 4.0, col + step, 0.0), axis=0, keepdims=True)
            return row

        stride = 2.0 * cap_l
        tr0 = by_half(first * stride + within[0], float(cap_l))
        tr1 = by_half(second * stride + within[1], float(cap_l))
        gr0, gr1 = by_half(lgates[:, 0:1], 0.0), by_half(lgates[:, 1:2], 0.0)
        ids = iota((experts * 2 * cap_l, experts * 8), 0)
        hit0, hit1 = ids == tr0, ids == tr1
        pick = jnp.where(hit0 | hit1, 1.0, 0.0).astype(bf16)
        scale = jnp.where(hit0, gr0, 0.0) + jnp.where(hit1, gr1, 0.0)
        high = scale.astype(bf16)
        low = (scale - high.astype(f32)).astype(bf16)
        wait_here(recv2.at[:, pl.ds(0, experts - 1)], l2_sem.at[1])
        inputs = recv2[0].reshape(experts * 8, LANES)
        cots = recv2[1].reshape(experts * 8, LANES)
        out3[0] = dot(pick, inputs).astype(bf16).reshape(experts, 2 * cap_l, LANES)
        out3[1] = (dot(high, cots) + dot(low, cots)).astype(bf16).reshape(experts, 2 * cap_l, LANES)
        for g in range(GROUPS):

            def send_l3(n, carry, g=g):
                j = lax.rem(n, 2) * (per // 2) + lax.div(n, 2) if per > 1 else n
                to = lax.rem(me + j * GROUPS + g, experts)
                rcopy(out3.at[:, to], recv3.at[:, g * per + j], l3_send, l3_recv.at[g], (sect, to, dp)).start()
                return carry

            lax.fori_loop(1 if g == 0 else 0, per, send_l3, 0)
        recv3[0, 0] = out3[0, me]
        recv3[1, 0] = out3[1, me]

        nx = shards // 2
        right, left = lax.rem(ring + 1, nx), lax.rem(ring + nx - 1, nx)

        def at_ring(position):
            return (sect, me, position * 2 + core)

        def gather(g):
            first_in = 1 if g == 0 else 0
            if per - first_in:
                wait_here(recv3.at[:, pl.ds(g * per + first_in, per - first_in)], l3_recv.at[g])
            for j in range(2):
                rows = recv3[j, g * per : (g + 1) * per].reshape(per * 2 * cap_l, LANES)
                block = dot(take_l_ref[...], rows).astype(bf16)
                xg4[g, core, ring, j] = jnp.concatenate([block[:group_slots], block[group_slots:]], axis=1)
            mine = xg4.at[g, core, ring]
            rcopy(mine, mine, l4_send.at[0, g], l4_recv.at[0, g], at_ring(right)).start()
            rcopy(mine, mine, l4_send.at[1, g], l4_recv.at[1, g], at_ring(left)).start()

        def relay(g):
            from_left, from_right = xg4.at[g, core, left], xg4.at[g, core, right]
            wait_here(from_left, l4_recv.at[0, g])
            on = from_left.at[0]
            rcopy(on, on, l4_send.at[2, g], l4_recv.at[2, g], at_ring(right)).start()
            wait_here(from_right, l4_recv.at[1, g])
            on = from_right.at[1]
            rcopy(on, on, l4_send.at[3, g], l4_recv.at[3, g], at_ring(left)).start()

        def share(g):
            across = xg4.at[g, core, lax.rem(ring + 2, nx)]
            wait_here(across.at[0], l4_recv.at[2, g])
            wait_here(across.at[1], l4_recv.at[3, g])
            mine = xg4.at[g, core]
            rcopy(mine, mine, l4_send.at[4, g], l4_recv.at[4, g], (sect, me, ring * 2 + 1 - core)).start()

        def hidden_parts(g):
            wait_here(xg4.at[g, 1 - core], l4_recv.at[4, g])
            pre = jnp.zeros((group_slots, hidden), f32)
            grad = jnp.zeros((group_slots, hidden), f32)
            for q in range(shards):
                cols = slice(q * part, (q + 1) * part)
                pre += dot_nt(xg4[g, q % 2, q // 2, 0], up_ref[:, cols])
                grad += dot_nt(xg4[g, q % 2, q // 2, 1], down_ref[:, cols])
            pre = pre * model_scale
            grad = grad * hidden_scale
            sig = 1.0 / (1.0 + jnp.exp(-pre))
            act_ref[g] = (pre * sig).astype(bf16)
            pre_ref[g] = (grad * sig * (1.0 + pre * (1.0 - sig))).astype(bf16)

        stages = (gather, relay, share, hidden_parts)
        for n in range(GROUPS + len(stages) - 1):
            for stage, run in enumerate(stages):
                if 0 <= n - stage < GROUPS:
                    run(n - stage)

        act = jnp.concatenate([act_ref[g] for g in range(GROUPS)], axis=0)
        pre = jnp.concatenate([pre_ref[g] for g in range(GROUPS)], axis=0)
        for j, (lhs, old, new, scale) in enumerate(
            ((pre, up_ref, fresh_up_ref, model_scale), (act, down_ref, fresh_down_ref, hidden_scale))
        ):
            for q in range(shards):
                cols = slice(q * part, (q + 1) * part)
                rhs = jnp.concatenate([xg4[g, q % 2, q // 2, j] for g in range(GROUPS)], axis=0)
                grad = dot_tn(lhs, rhs) * scale
                new[:, cols] = (old[:, cols].astype(f32) - step_size * grad).astype(bf16)
            rcopy(new, new, fresh_sem.at[j, 0], fresh_sem.at[j, 1], (other, me, dp)).start()

        for i in range(2):
            tables(i, i + 2)
        wait_here(states_ref, st_sem.at[1])
        for i in range(2):
            decode_step(i, i + 2, fresh_up_ref, fresh_down_ref)

        last = states_ref[...].astype(bf16)
        fin_src[...] = jnp.concatenate([last[:dec_rows], last[dec_rows:]], axis=1)
        half = shards // 2
        out_cols = pl.ds(pl.multiple_of(lax.rem(dp, half) * part, part), part)

        @pl.when(dp < half)
        def _():
            def send_far(q, carry):
                to = lax.rem(dp + q, shards)
                rcopy(fin_src, final_ref.at[:, out_cols], fin_sem.at[0], fin_sem.at[1], (other, me, to)).start()
                return carry

            lax.fori_loop(0, shards, send_far, 0)
            wait_here(final_ref, fin_sem.at[1])
            for _ in range(2):
                wait_sent(final_ref, fin_sem.at[0])

        @pl.when(dp >= half)
        def _():
            final_ref[:, out_cols] = fin_src[...]

            def send_near(q, carry):
                to = lax.rem(dp + q, shards)
                rcopy(fin_src, final_ref.at[:, out_cols], fin_sem.at[0], fin_sem.at[1], (sect, me, to)).start()
                return carry

            lax.fori_loop(1, shards, send_near, 0)
            wait_here(final_ref.at[:, pl.ds(0, (half - 1) * part)], fin_sem.at[1])
            wait_sent(final_ref, fin_sem.at[0])
            wait_sent(final_ref.at[:, pl.ds(0, (half - 1) * part)], fin_sem.at[0])

        for i in range(2):
            decode_sent(i)
        wait_sent(out2.at[:, pl.ds(0, experts - 1)], l2_sem.at[0])
        wait_sent(out3.at[:, pl.ds(0, experts - 1)], l3_send)
        for g in range(GROUPS):
            wait_sent(xg4.at[g, core, ring], l4_send.at[0, g])
            wait_sent(xg4.at[g, core, ring], l4_send.at[1, g])
            wait_sent(xg4.at[g, core, ring, 0], l4_send.at[2, g])
            wait_sent(xg4.at[g, core, ring, 1], l4_send.at[3, g])
            wait_sent(xg4.at[g, core], l4_send.at[4, g])
        wait_sent(fresh_up_ref, fresh_sem.at[0, 0])
        wait_sent(fresh_down_ref, fresh_sem.at[1, 0])


def on_device(
    decode_states, norm_gain, decode_routes, decode_gates, up_weight, down_weight,
    traj_inputs, traj_cotangents, traj_lengths, packing, learner_routes, learner_gates,
):
    experts, shards = lax.axis_size("exp"), lax.axis_size("dp")
    dec_rows, width = decode_states.shape
    lrn_rows = learner_routes.shape[0]
    part = width // shards
    hidden = up_weight.shape[2]
    cap_d = 3 * dec_rows * 2 // (2 * experts)
    cap_l = 3 * lrn_rows * 2 // (2 * experts)
    slots = experts * cap_d
    group_slots = experts // GROUPS * cap_l
    half_rows = traj_inputs.shape[1]
    vmem = pl.BlockSpec(memory_space=pltpu.VMEM)
    dma = pltpu.SemaphoreType.DMA
    final, fresh_up, fresh_down = pl.pallas_call(
        functools.partial(kernel, experts, shards, cap_d, cap_l),
        out_shape=(
            jax.ShapeDtypeStruct((dec_rows, width // 2), bf16),
            jax.ShapeDtypeStruct((hidden, width), bf16),
            jax.ShapeDtypeStruct((hidden, width), bf16),
        ),
        in_specs=[vmem] * 15,
        out_specs=(vmem,) * 3,
        scratch_shapes=[
            pltpu.VMEM((2, experts, 8, LANES), bf16),
            pltpu.VMEM((2, experts, 8, LANES), bf16),
            pltpu.VMEM((2, shards, slots, part), bf16),
            pltpu.VMEM((2, shards, slots, part), bf16),
            pltpu.VMEM((2, shards, slots, part), bf16),
            pltpu.VMEM((2, experts, 8, LANES), bf16),
            pltpu.VMEM((2, experts, 8, LANES), bf16),
            pltpu.VMEM((2 * dec_rows, LANES), f32),
            pltpu.VMEM((2, 2, 1, 2 * dec_rows), f32),
            pltpu.VMEM((2, 2, 2 * dec_rows, 1), f32),
            pltpu.VMEM((2, half_rows, part), bf16),
            pltpu.VMEM((2, experts, 8, LANES), bf16),
            pltpu.VMEM((2, experts, 8, LANES), bf16),
            pltpu.VMEM((2, experts, 2 * cap_l, LANES), bf16),
            pltpu.VMEM((2, experts, 2 * cap_l, LANES), bf16),
            pltpu.VMEM((GROUPS, 2, shards // 2, 2, group_slots, part), bf16),
            pltpu.VMEM((GROUPS, group_slots, hidden), bf16),
            pltpu.VMEM((GROUPS, group_slots, hidden), bf16),
            pltpu.VMEM((dec_rows, part), bf16),
            dma((4, 2, 2)),
            dma((2,)),
            dma((2,)),
            dma((2,)),
            dma((2,)),
            dma((2, 2)),
            dma,
            dma((GROUPS,)),
            dma((5, GROUPS)),
            dma((5, GROUPS)),
        ],
        compiler_params=pltpu.CompilerParams(
            collective_id=0, has_side_effects=True, vmem_limit_bytes=48 * 2**20
        ),
    )(
        decode_states, norm_gain.reshape(width // LANES, LANES), decode_routes, decode_gates,
        up_weight[0, 0], down_weight[0, 0], traj_inputs[0], traj_cotangents[0], traj_lengths[0], packing,
        learner_routes, learner_gates, *[jnp.asarray(m) for m in permutations(experts, cap_d, cap_l)],
    )
    return final, fresh_up[None, None], fresh_down[None, None]


def solution(mesh):
    in_specs = (
        P("exp", None),
        P(),
        P(None, "exp", None),
        P(None, "exp", None),
        P("sect", "exp", "dp", None),
        P("sect", "exp", "dp", None),
        P("sect", "exp", None),
        P("sect", "exp", None),
        P("exp", None, None),
        P("exp", None),
        P("exp", None),
        P("exp", None),
    )
    out_specs = (P("exp", "sect"), P("sect", "exp", "dp", None), P("sect", "exp", "dp", None))
    return jax.shard_map(on_device, mesh=mesh, in_specs=in_specs, out_specs=out_specs, check_vma=False)
```

time: 831 us -> 171 us (0.21)
  waiting for transfers between devices: 592 us -> 0 us
  Pallas kernels: 0 us -> 160 us
  starting transfers between devices: 111 us -> 0 us
  blocking collectives: 41.7 us -> 0 us
  local copies, waits for them, and re-layouts: 35.2 us -> 9.98 us
  other arithmetic: 16.6 us -> 0 us
  between operations: 14.4 us -> 0.72 us
  matrix products: 13.5 us -> 0 us
    all_to_all x9 -> x0, waiting for transfers between devices: 345 us -> none  [the longest x5 227 us: to_experts(): lax.all_to_all(payload, 'exp', split_axis=0, concat_axis=0, tiled=True)]
    psum x4 -> x0, waiting for transfers between devices: 246 us -> none  [sum_and_return(): summed = lax.psum(partial_out.astype(jnp.bfloat16), 'dp')]
    pallas_call x0 -> x1, Pallas kernels: none -> 160 us  [on_device(): pl.pallas_call(functools.partial(kernel, experts, shards, cap_d, cap_l),...]
    all_to_all x9 -> x0, starting transfers between devices: 87.9 us -> none  [the longest x5 44.1 us: to_experts(): lax.all_to_all(payload, 'exp', split_axis=0, concat_axis=0, tiled=True)]
    all_to_all x1 -> x0, blocking collectives: 41.7 us -> none  [sum_and_return(): lax.all_to_all(summed, 'exp', split_axis=0, concat_axis=0, tiled=True)]
    ppermute x3 -> x0, starting transfers between devices: 22.6 us -> none  [partner(): lax.ppermute(array, axis, [(i, i ^ 1 << apart) for i in range(lax.axis_si...]
    dot_general x14 -> x0, matrix products: 13.5 us -> none  [the longest x4 6.78 us: expert_forward(): jnp.einsum('sh,hd->sd', activated, down_slice, preferred_element_type=jnp...]
  transfers between devices with their start and end apart: 16 -> 0, of which waited for: 14 -> 0; matrix products, arithmetic and copies ran while one was open for 4% -> 0% of each run, Pallas kernels for 0% -> 0%
where the time goes in v1:
time: 171 us; the launch traced here: 170 us
  Pallas kernels  160 us (94%)
  local copies, waits for them, and re-layouts  9.98 us (6%)
    pallas_call x1, Pallas kernels, on_device(): pl.pallas_call(functools.partial(kernel, experts, shards, cap_d, cap_l),...  160 us
    unnamed x37, local copies, waits for them, and re-layouts  9.98 us

profile of v1, /device:TPU:1, one launch (start us, length us, event | category | flops | bytes accessed | tf_op | source)
XLA Modules:
  0.0 170.3 jit_solution(921887341559341096)
XLA Ops:
  0.6 0.0 copy-start.14
  0.6 0.0 copy-start.13
  0.7 0.0 copy-start.11
  0.7 0.7 copy-done.11
  1.4 0.1 copy.18.routes_ref
  1.5 0.1 copy.19.gates_ref
  1.6 0.1 copy.20.lroutes_ref
  1.7 0.0 copy-start.8
  1.7 0.0 copy-start.9
  1.7 0.0 copy-start.10
  1.7 0.1 copy.21.lgates_ref
  1.8 0.4 copy-done.2
  2.3 0.1 copy-done.3
  2.3 0.1 copy-done.8
  2.4 1.1 copy-done
  3.6 1.1 copy-done.1
  4.7 0.9 copy-done.4
  5.6 0.9 copy-done.5
  6.5 0.9 copy-done.6
  7.4 0.9 copy-done.7
  8.3 159.6 %shard_map.166 = (bf16[32,1024]{1,0:T(8,128)(2,1)S(1)}, bf16[192,2048]{1,0:T(8,128)(2,1)S(1)}, bf16[192,2048]{1,0:T(8,128)(2,1)S(1)}) custom-call(bf16[32,2048]{1,0:T(8,128)(2,1)S(1)} %copy-done.2, f32[16,128]{1,0:T(8,128)S(1)} %bitcast.14, s32[4,32,2]{2,1,0:T(8,128)S(1)} %copy.18.routes_ref, f32[4,32,2]{2,1,0:T(8,128)S(1)} %copy.19.gates_ref, ...), custom_call_target="tpu_custom_call" | custom-call | tf_op jit(solution)/shard_map/pallas_call | solution.py:461
  167.9 0.6 copy.25
  168.6 0.9 copy.26
  169.4 0.9 copy.27
  (14 shorter events, 0.0 us)
Async XLA Ops:
  0.6 1.1 copy-start.14
  0.6 0.9 copy-start.13
  0.7 0.7 copy-start.11
  0.7 0.8 copy-start.12
  1.4 0.9 copy-start.2
  1.4 1.0 copy-start.3
  1.7 0.7 copy-start.8
  1.7 0.7 copy-start.9
  1.7 0.7 copy-start.10
  2.4 1.1 copy-start
  3.6 1.1 copy-start.1
  4.7 0.9 copy-start.4
  5.6 0.9 copy-start.5
  6.5 0.9 copy-start.6
  7.4 0.9 copy-start.7

commit v2 on v1

v2 whole, which is shorter than its diff:
```python
import functools

import jax
import jax.numpy as jnp
from jax import lax
from jax.experimental import pallas as pl
from jax.experimental.pallas import tpu as pltpu
from jax.sharding import PartitionSpec as P

MESH = pl.DeviceIdType.MESH
step_size = 3.0
norm_eps = 1e-06
f32 = jnp.float32
bf16 = jnp.bfloat16
LANES = 128
GROUPS = 4


def dot(a, b):
    return lax.dot_general(a, b, (((1,), (0,)), ((), ())), preferred_element_type=f32)


def dot_nt(a, b):
    return lax.dot_general(a, b, (((1,), (1,)), ((), ())), preferred_element_type=f32)


def dot_tn(a, b):
    return lax.dot_general(a, b, (((0,), (0,)), ((), ())), preferred_element_type=f32)


def iota(shape, dim):
    return lax.broadcasted_iota(jnp.int32, shape, dim).astype(f32)


def to_row(col):
    n = col.shape[0]
    eye = iota((n, n), 0) == iota((n, n), 1)
    return jnp.sum(jnp.where(eye, col, 0.0), axis=0, keepdims=True)


def to_col(row):
    n = row.shape[1]
    eye = iota((n, n), 0) == iota((n, n), 1)
    return jnp.sum(jnp.where(eye, row, 0.0), axis=1, keepdims=True)


def ranks(first, second):
    n = first.shape[0]
    first_row, second_row = to_row(first), to_row(second)
    before = iota((n, n), 1) < iota((n, n), 0)
    out = []
    for mine in (first, second):
        same = ((first_row == mine) | (second_row == mine)) & before
        out.append(jnp.sum(jnp.where(same, 1.0, 0.0), axis=1, keepdims=True))
    return out


def far_first(count):
    return sorted(range(1, count), key=lambda k: (-min(k, count - k), k))


def slot_place(slot, per_source, block, c, half_step):
    source = jnp.floor((slot + 0.5) * (1.0 / per_source))
    return source * block + c * half_step + (slot - source * per_source)


def ones_where(condition):
    return jnp.where(condition, 1.0, 0.0).astype(bf16)


def kernel(
    experts, shards, cap_d, cap_l,
    rows_ref, gain_ref, routes_ref, gates_ref, up_ref, down_ref, in_ref, cot_ref, len_ref, pack_ref,
    lroutes_ref, lgates_ref,
    final_ref, fresh_up_ref, fresh_down_ref,
    d1_out, d1_in, xg, d3_out, d3_in, d4_out, d4_in, states_ref, trow_ref, tcol_ref, gcol_ref,
    held, out2, recv2, out3, recv3, xg4, act_ref, pre_ref, fin_src,
    up_v, down_v, rows_v, own_v, take_d, give_d, take_l,
    load_sem, dec_send, ends_recv, half_recv, l1_sem, l2_sem, st_sem, fin_sem, fresh_sem, l3_send, l3_recv, l4_send, l4_recv,
):
    sect, me, dp = lax.axis_index("sect"), lax.axis_index("exp"), lax.axis_index("dp")
    ring, core = lax.div(dp, 2), lax.rem(dp, 2)
    other = 1 - sect
    width = rows_ref.shape[1]
    part = width // shards
    hidden = up_ref.shape[0]
    model_scale = width ** (-0.5)
    hidden_scale = (hidden * shards) ** (-0.5)
    dec_rows = rows_ref.shape[0]
    slots = experts * cap_d
    per = experts // GROUPS
    group_slots = per * cap_l
    col0 = pl.multiple_of(dp * part, part)
    low, half = experts // 4, experts // 2
    half_slots = half * cap_d
    sect_far_first = far_first(experts)
    loads = [
        pltpu.make_async_copy(rows_ref.at[:, pl.ds(col0, part)], rows_v, load_sem.at[0]),
        pltpu.make_async_copy(in_ref.at[:, pl.ds(col0, part)], own_v.at[0], load_sem.at[1]),
        pltpu.make_async_copy(cot_ref.at[:, pl.ds(col0, part)], own_v.at[1], load_sem.at[2]),
        pltpu.make_async_copy(up_ref, up_v, load_sem.at[3]),
        pltpu.make_async_copy(down_ref, down_v, load_sem.at[4]),
    ]

    def rcopy(src, dst, send, recv, device):
        return pltpu.make_async_remote_copy(
            src_ref=src, dst_ref=dst, send_sem=send, recv_sem=recv, device_id=device, device_id_type=MESH
        )

    def wait_sent(ref, sem):
        rcopy(ref, ref, sem, sem, (sect, me, dp)).wait_send()

    def wait_here(ref, sem):
        rcopy(ref, ref, sem, sem, (sect, me, dp)).wait_recv()

    barrier = pltpu.get_barrier_semaphore()

    for k in sect_far_first:
        pl.semaphore_signal(barrier, inc=1, device_id=(sect, lax.rem(me + k, experts), dp), device_id_type=MESH)
    for q in range(1, shards):
        pl.semaphore_signal(barrier, inc=1, device_id=(sect, me, lax.rem(dp + q, shards)), device_id_type=MESH)
    for q in range(shards):
        pl.semaphore_signal(barrier, inc=1, device_id=(other, me, lax.rem(dp + q, shards)), device_id_type=MESH)
    for load in loads:
        load.start()
    for c in range(2):
        row, col = iota((half_slots, half * 8), 0), iota((half_slots, half * 8), 1)
        take_d[c] = ones_where(col == slot_place(row, cap_d, 8.0, c, 4.0))
        row, col = iota((half * 8, half_slots), 0), iota((half * 8, half_slots), 1)
        give_d[c] = ones_where(row == slot_place(col, cap_d, 8.0, c, 4.0))
        row, col = iota((group_slots, 2 * group_slots), 0), iota((group_slots, 2 * group_slots), 1)
        take_l[c] = ones_where(col == slot_place(row, cap_l, 2.0 * cap_l, c, float(cap_l)))

    def greeted():
        pl.semaphore_wait(barrier, experts - 1 + shards - 1 + shards)

    def tables(i, t):
        routes = routes_ref[t].astype(f32)
        first, second = to_col(routes[0:1]), to_col(routes[1:2])
        within = ranks(first, second)
        for k, mine in enumerate((first, second)):
            target = mine * 8.0 + within[k]
            both = jnp.concatenate([target, target + 4.0], axis=0)
            tcol_ref[i, k] = both
            trow_ref[i, k] = to_row(both)
        for k in range(2):
            gate = to_col(gates_ref[t, k : k + 1, :])
            gcol_ref[i, k] = jnp.concatenate([gate, gate], axis=0)

    def decode_step(i, t, up, down):
        gain0, gain1 = gain_ref[pl.ds(2 * dp, 1), :], gain_ref[pl.ds(2 * dp + 1, 1), :]
        gains = jnp.concatenate(
            [jnp.broadcast_to(gain0, (dec_rows, LANES)), jnp.broadcast_to(gain1, (dec_rows, LANES))], axis=0
        )
        y = (states_ref[...] * gains).astype(bf16)
        row_ids = iota((experts * 8, 2 * dec_rows), 0)
        pick = (row_ids == trow_ref[i, 0]) | (row_ids == trow_ref[i, 1])
        pick = jnp.where(pick, 1.0, 0.0).astype(bf16)
        d1_out[i] = dot(pick, y).astype(bf16).reshape(experts, 8, LANES)
        for k in sect_far_first:
            place = (k - low) % experts
            to = lax.rem(me + k, experts)
            arrival = half_recv.at[0, i, place // half]
            rcopy(d1_out.at[i, to], d1_in.at[i, place], dec_send.at[0, i], arrival, (sect, to, dp)).start()
        own_place = experts - low
        d1_in[i, own_place] = d1_out[i, me]

        def gather(h):
            wait_here(d1_in.at[i, pl.ds(h * half, half - h)], half_recv.at[0, i, h])
            arrived = d1_in[i, h * half : (h + 1) * half].reshape(half * 8, LANES)
            block = [dot(take_d[c], arrived).astype(bf16) for c in range(2)]
            xg[i, h, dp] = jnp.concatenate(block, axis=1)
            mine = xg.at[i, h, dp]
            for q in far_first(shards):
                to = lax.rem(dp + q, shards)
                rcopy(mine, mine, dec_send.at[1 + h, i], half_recv.at[1, i, h], (sect, me, to)).start()

        def up_part(h):
            wait_here(xg.at[i, h, pl.ds(0, shards - 1)], half_recv.at[1, i, h])
            before_act = jnp.zeros((half_slots, hidden), f32)
            squares = jnp.zeros((half_slots, part), f32)
            for q in range(shards):
                piece = xg[i, h, q]
                before_act += dot_nt(piece, up[:, q * part : (q + 1) * part])
                gain = jnp.concatenate([gain_ref[2 * q : 2 * q + 1], gain_ref[2 * q + 1 : 2 * q + 2]], axis=1)
                wide = piece.astype(f32) * (1.0 / gain)
                squares += wide * wide
            mean = jnp.sum(squares, axis=1, keepdims=True) * (1.0 / width)
            before_act = before_act * (lax.rsqrt(mean + norm_eps) * model_scale)
            return (before_act / (1.0 + jnp.exp(-before_act))).astype(bf16)

        def down_part(h, act):
            for q in range(shards):
                d3_out[i, h, q] = (dot(act, down[:, q * part : (q + 1) * part]) * hidden_scale).astype(bf16)
            for q in far_first(shards):
                to = lax.rem(dp + q, shards)
                rcopy(
                    d3_out.at[i, h, to], d3_in.at[i, h, dp], dec_send.at[3 + h, i], half_recv.at[2, i, h], (sect, me, to)
                ).start()
            d3_in[i, h, dp] = d3_out[i, h, dp]

        def give_back(h):
            wait_here(d3_in.at[i, h, pl.ds(0, shards - 1)], half_recv.at[2, i, h])
            total = d3_in[i, h, 0].astype(f32)
            for q in range(1, shards):
                total += d3_in[i, h, q].astype(f32)
            total = total.astype(bf16)
            back = dot(give_d[0], total[:, :LANES]) + dot(give_d[1], total[:, LANES:])
            d4_out[i, h * half : (h + 1) * half] = back.astype(bf16).reshape(half, 8, LANES)
            for k in sect_far_first:
                place = (k - low) % experts
                if place // half == h:
                    to = lax.rem(me + experts - k, experts)
                    rcopy(d4_out.at[i, place], d4_in.at[i, me], dec_send.at[5, i], ends_recv.at[i], (sect, to, dp)).start()

        gather(1)
        gather(0)
        near_act = up_part(1)
        down_part(0, up_part(0))
        down_part(1, near_act)
        give_back(0)
        give_back(1)
        d4_in[i, me] = d4_out[i, own_place]
        lane_ids = iota((2 * dec_rows, experts * 8), 1)
        mix = jnp.where(lane_ids == tcol_ref[i, 0], gcol_ref[i, 0], 0.0)
        mix += jnp.where(lane_ids == tcol_ref[i, 1], gcol_ref[i, 1], 0.0)
        high = mix.astype(bf16)
        rest = mix - high.astype(f32)
        middle = rest.astype(bf16)
        low_part = (rest - middle.astype(f32)).astype(bf16)
        wait_here(d4_in.at[i, pl.ds(0, experts - 1)], ends_recv.at[i])
        returned = d4_in[i].reshape(experts * 8, LANES)
        states_ref[...] += dot(high, returned) + (dot(middle, returned) + dot(low_part, returned))

    def decode_sent(i):
        wait_sent(d1_out.at[i, pl.ds(0, experts - 1)], dec_send.at[0, i])
        for h in range(2):
            wait_sent(xg.at[i, h, pl.ds(0, shards - 1)], dec_send.at[1 + h, i])
            wait_sent(d3_out.at[i, h, pl.ds(0, shards - 1)], dec_send.at[3 + h, i])
        wait_sent(d4_out.at[i, pl.ds(0, experts - 1)], dec_send.at[5, i])

    @pl.when(sect == 0)
    def _():
        for i in range(2):
            tables(i, i)
        loads[0].wait()
        rows = rows_v[...].astype(f32)
        states_ref[...] = jnp.concatenate([rows[:, :LANES], rows[:, LANES:]], axis=0)
        loads[1].wait()
        loads[2].wait()
        greeted()
        rcopy(own_v, held, l1_sem.at[0], l1_sem.at[1], (other, me, dp)).start()
        loads[3].wait()
        loads[4].wait()
        for i in range(2):
            decode_step(i, i, up_v, down_v)
        move = rcopy(states_ref, states_ref, st_sem.at[0], st_sem.at[1], (other, me, dp))
        move.start()
        move.wait_send()
        wait_sent(held, l1_sem.at[0])
        for i in range(2):
            decode_sent(i)
        wait_here(fresh_up_ref, fresh_sem.at[0, 1])
        wait_here(fresh_down_ref, fresh_sem.at[1, 1])
        wait_here(final_ref, fin_sem.at[1])

    @pl.when(sect == 1)
    def _():
        lengths = len_ref[...].astype(f32)
        count = lengths.shape[1]
        length = jnp.concatenate([to_col(lengths[0:1]), to_col(lengths[1:2])], axis=0)
        both = 2 * count
        a, b = iota((both, both), 0), iota((both, both), 1)
        same_half = (a < count) == (b < count)
        start_row = jnp.sum(jnp.where(same_half & (a < b), length, 0.0), axis=0, keepdims=True)
        length_row = to_row(length)
        half_rows = held.shape[1]
        r, t = iota((2 * half_rows, both), 0), iota((2 * half_rows, both), 1)
        second = r >= half_rows
        row_in = r - jnp.where(second, float(half_rows), 0.0)
        offset = row_in - start_row
        inside = (second == (t >= count)) & (offset >= 0.0) & (offset < length_row)
        shard = pack_ref[...].astype(f32)
        target2 = jnp.sum(jnp.where(inside, shard * 8.0 + offset, 0.0), axis=1, keepdims=True)
        target2 = to_row(jnp.concatenate([target2, target2 + 4.0], axis=0))
        row_ids = iota((experts * 8, 4 * half_rows), 0)
        pack = ones_where(row_ids == target2)
        for load in loads:
            load.wait()
        for i in range(2):
            tables(i, i + 2)
        greeted()
        wait_here(held, l1_sem.at[1])
        for j in range(2):
            far, own = held[j], own_v[j]
            stacked = jnp.concatenate([far[:, :LANES], own[:, :LANES], far[:, LANES:], own[:, LANES:]], axis=0)
            out2[j] = dot(pack, stacked).astype(bf16).reshape(experts, 8, LANES)
            recv2[j, me] = out2[j, me]

        for k in sect_far_first:
            to = lax.rem(me + k, experts)
            rcopy(out2.at[:, to], recv2.at[:, me], l2_sem.at[0], l2_sem.at[1], (sect, to, dp)).start()

        lroutes = lroutes_ref[...].astype(f32)
        first, second = to_col(lroutes[0:1]), to_col(lroutes[1:2])
        within = ranks(first, second)
        gates = [to_col(lgates_ref[k : k + 1, :]) for k in range(2)]

        def by_half(col, step):
            n = col.shape[0]
            row = jnp.zeros((1, 2 * n), f32)
            r, l = iota((n, 2 * n), 0), iota((n, 2 * n), 1)
            source = jnp.floor(r * 0.25)
            place = source * 4.0 + r
            row += jnp.sum(jnp.where(l == place, col, 0.0), axis=0, keepdims=True)
            row += jnp.sum(jnp.where(l == place + 4.0, col + step, 0.0), axis=0, keepdims=True)
            return row

        stride = 2.0 * cap_l
        tr0 = by_half(first * stride + within[0], float(cap_l))
        tr1 = by_half(second * stride + within[1], float(cap_l))
        gr0, gr1 = by_half(gates[0], 0.0), by_half(gates[1], 0.0)
        ids = iota((experts * 2 * cap_l, experts * 8), 0)
        hit0, hit1 = ids == tr0, ids == tr1
        pick = ones_where(hit0 | hit1)
        scale = jnp.where(hit0, gr0, 0.0) + jnp.where(hit1, gr1, 0.0)
        high = scale.astype(bf16)
        low = (scale - high.astype(f32)).astype(bf16)
        wait_here(recv2.at[:, pl.ds(0, experts - 1)], l2_sem.at[1])
        inputs = recv2[0].reshape(experts * 8, LANES)
        cots = recv2[1].reshape(experts * 8, LANES)
        out3[0] = dot(pick, inputs).astype(bf16).reshape(experts, 2 * cap_l, LANES)
        out3[1] = (dot(high, cots) + dot(low, cots)).astype(bf16).reshape(experts, 2 * cap_l, LANES)
        for g in range(GROUPS):
            for k in sect_far_first:
                if k % GROUPS == g:
                    to = lax.rem(me + k, experts)
                    place = g * per + k // GROUPS
                    rcopy(out3.at[:, to], recv3.at[:, place], l3_send, l3_recv.at[g], (sect, to, dp)).start()
        recv3[0, 0] = out3[0, me]
        recv3[1, 0] = out3[1, me]

        nx = shards // 2
        right, left = lax.rem(ring + 1, nx), lax.rem(ring + nx - 1, nx)

        def at_ring(position):
            return (sect, me, position * 2 + core)

        def spread(g):
            first_in = 1 if g == 0 else 0
            if per - first_in:
                wait_here(recv3.at[:, pl.ds(g * per + first_in, per - first_in)], l3_recv.at[g])
            for j in range(2):
                rows = recv3[j, g * per : (g + 1) * per].reshape(per * 2 * cap_l, LANES)
                block = [dot(take_l[c], rows).astype(bf16) for c in range(2)]
                xg4[g, core, ring, j] = jnp.concatenate(block, axis=1)
            mine = xg4.at[g, core, ring]
            rcopy(mine, mine, l4_send.at[0, g], l4_recv.at[0, g], at_ring(right)).start()
            rcopy(mine, mine, l4_send.at[1, g], l4_recv.at[1, g], at_ring(left)).start()

        def relay(g):
            from_left, from_right = xg4.at[g, core, left], xg4.at[g, core, right]
            wait_here(from_left, l4_recv.at[0, g])
            on = from_left.at[0]
            rcopy(on, on, l4_send.at[2, g], l4_recv.at[2, g], at_ring(right)).start()
            wait_here(from_right, l4_recv.at[1, g])
            on = from_right.at[1]
            rcopy(on, on, l4_send.at[3, g], l4_recv.at[3, g], at_ring(left)).start()

        def share(g):
            across = xg4.at[g, core, lax.rem(ring + 2, nx)]
            wait_here(across.at[0], l4_recv.at[2, g])
            wait_here(across.at[1], l4_recv.at[3, g])
            mine = xg4.at[g, core]
            rcopy(mine, mine, l4_send.at[4, g], l4_recv.at[4, g], (sect, me, ring * 2 + 1 - core)).start()

        def hidden_parts(g):
            wait_here(xg4.at[g, 1 - core], l4_recv.at[4, g])
            pre = jnp.zeros((group_slots, hidden), f32)
            grad = jnp.zeros((group_slots, hidden), f32)
            for q in range(shards):
                cols = slice(q * part, (q + 1) * part)
                pre += dot_nt(xg4[g, q % 2, q // 2, 0], up_v[:, cols])
                grad += dot_nt(xg4[g, q % 2, q // 2, 1], down_v[:, cols])
            pre = pre * model_scale
            grad = grad * hidden_scale
            sig = 1.0 / (1.0 + jnp.exp(-pre))
            act_ref[g] = (pre * sig).astype(bf16)
            pre_ref[g] = (grad * sig * (1.0 + pre * (1.0 - sig))).astype(bf16)

        stages = (spread, relay, share, hidden_parts)
        for n in range(GROUPS + len(stages) - 1):
            for stage, run in enumerate(stages):
                if 0 <= n - stage < GROUPS:
                    run(n - stage)

        act = jnp.concatenate([act_ref[g] for g in range(GROUPS)], axis=0)
        pre = jnp.concatenate([pre_ref[g] for g in range(GROUPS)], axis=0)
        for j, (lhs, old, new, scale) in enumerate(
            ((pre, up_v, fresh_up_ref, model_scale), (act, down_v, fresh_down_ref, hidden_scale))
        ):
            for q in range(shards):
                cols = slice(q * part, (q + 1) * part)
                rhs = jnp.concatenate([xg4[g, q % 2, q // 2, j] for g in range(GROUPS)], axis=0)
                grad = dot_tn(lhs, rhs) * scale
                new[:, cols] = (old[:, cols].astype(f32) - step_size * grad).astype(bf16)
            rcopy(new, new, fresh_sem.at[j, 0], fresh_sem.at[j, 1], (other, me, dp)).start()

        wait_here(states_ref, st_sem.at[1])
        for i in range(2):
            decode_step(i, i + 2, fresh_up_ref, fresh_down_ref)

        last = states_ref[...].astype(bf16)
        fin_src[...] = jnp.concatenate([last[:dec_rows], last[dec_rows:]], axis=1)
        near = shards // 2
        out_cols = pl.ds(pl.multiple_of(lax.rem(dp, near) * part, part), part)

        @pl.when(dp < near)
        def _():
            def send_far(q, carry):
                to = lax.rem(dp + q, shards)
                rcopy(fin_src, final_ref.at[:, out_cols], fin_sem.at[0], fin_sem.at[1], (other, me, to)).start()
                return carry

            lax.fori_loop(0, shards, send_far, 0)
            wait_here(final_ref, fin_sem.at[1])
            for _ in range(2):
                wait_sent(final_ref, fin_sem.at[0])

        @pl.when(dp >= near)
        def _():
            final_ref[:, out_cols] = fin_src[...]

            def send_near(q, carry):
                to = lax.rem(dp + q, shards)
                rcopy(fin_src, final_ref.at[:, out_cols], fin_sem.at[0], fin_sem.at[1], (sect, me, to)).start()
                return carry

            lax.fori_loop(1, shards, send_near, 0)
            wait_here(final_ref.at[:, pl.ds(0, (near - 1) * part)], fin_sem.at[1])
            wait_sent(final_ref, fin_sem.at[0])
            wait_sent(final_ref.at[:, pl.ds(0, (near - 1) * part)], fin_sem.at[0])

        for i in range(2):
            decode_sent(i)
        wait_sent(out2.at[:, pl.ds(0, experts - 1)], l2_sem.at[0])
        wait_sent(out3.at[:, pl.ds(0, experts - 1)], l3_send)
        for g in range(GROUPS):
            wait_sent(xg4.at[g, core, ring], l4_send.at[0, g])
            wait_sent(xg4.at[g, core, ring], l4_send.at[1, g])
            wait_sent(xg4.at[g, core, ring, 0], l4_send.at[2, g])
            wait_sent(xg4.at[g, core, ring, 1], l4_send.at[3, g])
            wait_sent(xg4.at[g, core], l4_send.at[4, g])
        wait_sent(fresh_up_ref, fresh_sem.at[0, 0])
        wait_sent(fresh_down_ref, fresh_sem.at[1, 0])


def on_device(
    decode_states, norm_gain, decode_routes, decode_gates, up_weight, down_weight,
    traj_inputs, traj_cotangents, traj_lengths, packing, learner_routes, learner_gates,
):
    experts, shards = lax.axis_size("exp"), lax.axis_size("dp")
    dec_rows, width = decode_states.shape
    lrn_rows = learner_routes.shape[0]
    part = width // shards
    hidden = up_weight.shape[2]
    cap_d = 3 * dec_rows * 2 // (2 * experts)
    cap_l = 3 * lrn_rows * 2 // (2 * experts)
    slots = experts * cap_d
    group_slots = experts // GROUPS * cap_l
    half_rows = traj_inputs.shape[1]
    vmem = pl.BlockSpec(memory_space=pltpu.VMEM)
    hbm = pl.BlockSpec(memory_space=pltpu.HBM)
    dma = pltpu.SemaphoreType.DMA
    final, fresh_up, fresh_down = pl.pallas_call(
        functools.partial(kernel, experts, shards, cap_d, cap_l),
        out_shape=(
            jax.ShapeDtypeStruct((dec_rows, width // 2), bf16),
            jax.ShapeDtypeStruct((hidden, width), bf16),
            jax.ShapeDtypeStruct((hidden, width), bf16),
        ),
        in_specs=[hbm, vmem, vmem, vmem, hbm, hbm, hbm, hbm, vmem, vmem, vmem, vmem],
        out_specs=(vmem,) * 3,
        scratch_shapes=[
            pltpu.VMEM((2, experts, 8, LANES), bf16),
            pltpu.VMEM((2, experts, 8, LANES), bf16),
            pltpu.VMEM((2, 2, shards, slots // 2, part), bf16),
            pltpu.VMEM((2, 2, shards, slots // 2, part), bf16),
            pltpu.VMEM((2, 2, shards, slots // 2, part), bf16),
            pltpu.VMEM((2, experts, 8, LANES), bf16),
            pltpu.VMEM((2, experts, 8, LANES), bf16),
            pltpu.VMEM((2 * dec_rows, LANES), f32),
            pltpu.VMEM((2, 2, 1, 2 * dec_rows), f32),
            pltpu.VMEM((2, 2, 2 * dec_rows, 1), f32),
            pltpu.VMEM((2, 2, 2 * dec_rows, 1), f32),
            pltpu.VMEM((2, half_rows, part), bf16),
            pltpu.VMEM((2, experts, 8, LANES), bf16),
            pltpu.VMEM((2, experts, 8, LANES), bf16),
            pltpu.VMEM((2, experts, 2 * cap_l, LANES), bf16),
            pltpu.VMEM((2, experts, 2 * cap_l, LANES), bf16),
            pltpu.VMEM((GROUPS, 2, shards // 2, 2, group_slots, part), bf16),
            pltpu.VMEM((GROUPS, group_slots, hidden), bf16),
            pltpu.VMEM((GROUPS, group_slots, hidden), bf16),
            pltpu.VMEM((dec_rows, part), bf16),
            pltpu.VMEM((hidden, width), bf16),
            pltpu.VMEM((hidden, width), bf16),
            pltpu.VMEM((dec_rows, part), bf16),
            pltpu.VMEM((2, half_rows, part), bf16),
            pltpu.VMEM((2, slots // 2, experts * 4), bf16),
            pltpu.VMEM((2, experts * 4, slots // 2), bf16),
            pltpu.VMEM((2, group_slots, 2 * group_slots), bf16),
            dma((5,)),
            dma((6, 2)),
            dma((2,)),
            dma((3, 2, 2)),
            dma((2,)),
            dma((2,)),
            dma((2,)),
            dma((2,)),
            dma((2, 2)),
            dma,
            dma((GROUPS,)),
            dma((5, GROUPS)),
            dma((5, GROUPS)),
        ],
        compiler_params=pltpu.CompilerParams(
            collective_id=0, has_side_effects=True, vmem_limit_bytes=56 * 2**20
        ),
    )(
        decode_states, norm_gain.reshape(width // LANES, LANES),
        decode_routes.transpose(0, 2, 1), decode_gates.transpose(0, 2, 1),
        up_weight[0, 0], down_weight[0, 0], traj_inputs[0], traj_cotangents[0], traj_lengths[0], packing,
        learner_routes.T, learner_gates.T,
    )
    return final, fresh_up[None, None], fresh_down[None, None]


def solution(mesh):
    in_specs = (
        P("exp", None),
        P(),
        P(None, "exp", None),
        P(None, "exp", None),
        P("sect", "exp", "dp", None),
        P("sect", "exp", "dp", None),
        P("sect", "exp", None),
        P("sect", "exp", None),
        P("exp", None, None),
        P("exp", None),
        P("exp", None),
        P("exp", None),
    )
    out_specs = (P("exp", "sect"), P("sect", "exp", "dp", None), P("sect", "exp", "dp", None))
    return jax.shard_map(on_device, mesh=mesh, in_specs=in_specs, out_specs=out_specs, check_vma=False)
```

time: 171 us -> 155 us (0.906)
  Pallas kernels: 160 us -> 149 us
  local copies, waits for them, and re-layouts: 9.98 us -> 4.52 us
    pallas_call x1, Pallas kernels: 160 us -> 149 us  [on_device(): pl.pallas_call(functools.partial(kernel, experts, shards, cap_d, cap_l),...]
    unnamed x37 -> x5, local copies, waits for them, and re-layouts: 9.98 us -> 4.52 us
where the time goes in v2:
time: 155 us
  Pallas kernels  149 us (96%)
  local copies, waits for them, and re-layouts  4.52 us (3%)
    pallas_call x1, Pallas kernels, on_device(): pl.pallas_call(functools.partial(kernel, experts, shards, cap_d, cap_l),...  149 us
    unnamed x5, local copies, waits for them, and re-layouts  4.52 us

profile of v2, /device:TPU:1, one launch (start us, length us, event | category | flops | bytes accessed | tf_op | source)
XLA Modules:
  0.0 154.5 jit_solution(17223519795018452459)
XLA Ops:
  0.6 149.4 %shard_map.139 = (bf16[32,1024]{1,0:T(8,128)(2,1)}, bf16[192,2048]{1,0:T(8,128)(2,1)}, bf16[192,2048]{1,0:T(8,128)(2,1)}) custom-call(bf16[32,2048]{1,0:T(8,128)(2,1)} %rows_ref.1, f32[16,128]{1,0:T(8,128)} %bitcast.18, s32[4,2,32]{2,1,0:T(2,128)} %bitcast.19, f32[4,2,32]{2,1,0:T(2,128)} %bitcast.20, bf16[192,2048]{1,0:T(8,128)(2,1)} %bitcast.12, ...), custom_call_target="tpu_custom_call" | custom-call | tf_op jit(solution)/shard_map/pallas_call | solution.py:475
  150.0 1.5 copy.18
  151.5 0.0 copy-start
  151.5 2.2 %copy.19 = bf16[1,1,192,2048]{3,2,1,0:T(8,128)(2,1)} copy(bf16[1,1,192,2048]{3,2,1,0:T(8,128)(2,1)} %bitcast.15) | data formatting | bytes 1572864
  153.7 0.0 copy-done
  153.7 0.9 copy.20
Async XLA Ops:
  151.5 2.2 %copy-start = (bf16[192,2048]{1,0:T(8,128)(2,1)S(1)}, bf16[192,2048]{1,0:T(8,128)(2,1)}, u32[]{:S(2)}) copy-start(bf16[192,2048]{1,0:T(8,128)(2,1)} %get-tuple-element.8) | copy-start | bytes 2359300

commit v3 on v2

--- a/solution.py
+++ b/solution.py
@@ -73,9 +73,9 @@
     rows_ref, gain_ref, routes_ref, gates_ref, up_ref, down_ref, in_ref, cot_ref, len_ref, pack_ref,
     lroutes_ref, lgates_ref,
     final_ref, fresh_up_ref, fresh_down_ref,
-    d1_out, d1_in, xg, d3_out, d3_in, d4_out, d4_in, states_ref, trow_ref, tcol_ref, gcol_ref,
+    d1_out, d1_in, xg_far, xg_near, d3_out_far, d3_out_near, d3_in_far, d3_in_near, d4_out, d4_in, states_ref, trow_ref, tcol_ref, gcol_ref,
     held, out2, recv2, out3, recv3, xg4, act_ref, pre_ref, fin_src,
-    up_v, down_v, rows_v, own_v, take_d, give_d, take_l,
+    up_v, down_v, rows_v, own_v, take_far, take_near, give_far, give_near, take_l,
     load_sem, dec_send, ends_recv, half_recv, l1_sem, l2_sem, st_sem, fin_sem, fresh_sem, l3_send, l3_recv, l4_send, l4_recv,
 ):
     sect, me, dp = lax.axis_index("sect"), lax.axis_index("exp"), lax.axis_index("dp")
@@ -87,12 +87,14 @@
     model_scale = width ** (-0.5)
     hidden_scale = (hidden * shards) ** (-0.5)
     dec_rows = rows_ref.shape[0]
-    slots = experts * cap_d
     per = experts // GROUPS
     group_slots = per * cap_l
     col0 = pl.multiple_of(dp * part, part)
-    low, half = experts // 4, experts // 2
-    half_slots = half * cap_d
+    sizes = (experts // 4, experts - experts // 4)
+    firsts = (0, sizes[0])
+    low = (experts - sizes[0] + 1) // 2
+    xg, d3_out, d3_in = (xg_far, xg_near), (d3_out_far, d3_out_near), (d3_in_far, d3_in_near)
+    take_d, give_d = (take_far, take_near), (give_far, give_near)
     sect_far_first = far_first(experts)
     loads = [
         pltpu.make_async_copy(rows_ref.at[:, pl.ds(col0, part)], rows_v, load_sem.at[0]),
@@ -117,6 +119,8 @@
 
     for k in sect_far_first:
         pl.semaphore_signal(barrier, inc=1, device_id=(sect, lax.rem(me + k, experts), dp), device_id_type=MESH)
+    for k in sect_far_first:
+        pl.semaphore_signal(barrier, inc=1, device_id=(other, lax.rem(me + k, experts), dp), device_id_type=MESH)
     for q in range(1, shards):
         pl.semaphore_signal(barrier, inc=1, device_id=(sect, me, lax.rem(dp + q, shards)), device_id_type=MESH)
     for q in range(shards):
@@ -124,15 +128,16 @@
     for load in loads:
         load.start()
     for c in range(2):
-        row, col = iota((half_slots, half * 8), 0), iota((half_slots, half * 8), 1)
-        take_d[c] = ones_where(col == slot_place(row, cap_d, 8.0, c, 4.0))
-        row, col = iota((half * 8, half_slots), 0), iota((half * 8, half_slots), 1)
-        give_d[c] = ones_where(row == slot_place(col, cap_d, 8.0, c, 4.0))
+        for h, size in enumerate(sizes):
+            row, col = iota((size * cap_d, size * 8), 0), iota((size * cap_d, size * 8), 1)
+            take_d[h][c] = ones_where(col == slot_place(row, cap_d, 8.0, c, 4.0))
+            row, col = iota((size * 8, size * cap_d), 0), iota((size * 8, size * cap_d), 1)
+            give_d[h][c] = ones_where(row == slot_place(col, cap_d, 8.0, c, 4.0))
         row, col = iota((group_slots, 2 * group_slots), 0), iota((group_slots, 2 * group_slots), 1)
         take_l[c] = ones_where(col == slot_place(row, cap_l, 2.0 * cap_l, c, float(cap_l)))
 
     def greeted():
-        pl.semaphore_wait(barrier, experts - 1 + shards - 1 + shards)
+        pl.semaphore_wait(barrier, 2 * (experts - 1) + shards - 1 + shards)
 
     def tables(i, t):
         routes = routes_ref[t].astype(f32)
@@ -147,7 +152,7 @@
             gate = to_col(gates_ref[t, k : k + 1, :])
             gcol_ref[i, k] = jnp.concatenate([gate, gate], axis=0)
 
-    def decode_step(i, t, up, down):
+    def decode_step(i, up, down, meanwhile=None, hand_over=False):
         gain0, gain1 = gain_ref[pl.ds(2 * dp, 1), :], gain_ref[pl.ds(2 * dp + 1, 1), :]
         gains = jnp.concatenate(
             [jnp.broadcast_to(gain0, (dec_rows, LANES)), jnp.broadcast_to(gain1, (dec_rows, LANES))], axis=0
@@ -160,27 +165,28 @@
         for k in sect_far_first:
             place = (k - low) % experts
             to = lax.rem(me + k, experts)
-            arrival = half_recv.at[0, i, place // half]
+            arrival = half_recv.at[0, i, 0 if place < sizes[0] else 1]
             rcopy(d1_out.at[i, to], d1_in.at[i, place], dec_send.at[0, i], arrival, (sect, to, dp)).start()
         own_place = experts - low
         d1_in[i, own_place] = d1_out[i, me]
 
         def gather(h):
-            wait_here(d1_in.at[i, pl.ds(h * half, half - h)], half_recv.at[0, i, h])
-            arrived = d1_in[i, h * half : (h + 1) * half].reshape(half * 8, LANES)
-            block = [dot(take_d[c], arrived).astype(bf16) for c in range(2)]
-            xg[i, h, dp] = jnp.concatenate(block, axis=1)
-            mine = xg.at[i, h, dp]
+            first, size = firsts[h], sizes[h]
+            wait_here(d1_in.at[i, pl.ds(first, size - h)], half_recv.at[0, i, h])
+            arrived = d1_in[i, first : first + size].reshape(size * 8, LANES)
+            block = [dot(take_d[h][c], arrived).astype(bf16) for c in range(2)]
+            xg[h][i, dp] = jnp.concatenate(block, axis=1)
+            mine = xg[h].at[i, dp]
             for q in far_first(shards):
                 to = lax.rem(dp + q, shards)
                 rcopy(mine, mine, dec_send.at[1 + h, i], half_recv.at[1, i, h], (sect, me, to)).start()
 
         def up_part(h):
-            wait_here(xg.at[i, h, pl.ds(0, shards - 1)], half_recv.at[1, i, h])
-            before_act = jnp.zeros((half_slots, hidden), f32)
-            squares = jnp.zeros((half_slots, part), f32)
+            wait_here(xg[h].at[i, pl.ds(0, shards - 1)], half_recv.at[1, i, h])
+            before_act = jnp.zeros((sizes[h] * cap_d, hidden), f32)
+            squares = jnp.zeros((sizes[h] * cap_d, part), f32)
             for q in range(shards):
-                piece = xg[i, h, q]
+                piece = xg[h][i, q]
                 before_act += dot_nt(piece, up[:, q * part : (q + 1) * part])
                 gain = jnp.concatenate([gain_ref[2 * q : 2 * q + 1], gain_ref[2 * q + 1 : 2 * q + 2]], axis=1)
                 wide = piece.astype(f32) * (1.0 / gain)
@@ -191,53 +197,62 @@
 
         def down_part(h, act):
             for q in range(shards):
-                d3_out[i, h, q] = (dot(act, down[:, q * part : (q + 1) * part]) * hidden_scale).astype(bf16)
+                d3_out[h][i, q] = (dot(act, down[:, q * part : (q + 1) * part]) * hidden_scale).astype(bf16)
             for q in far_first(shards):
                 to = lax.rem(dp + q, shards)
-                rcopy(
-                    d3_out.at[i, h, to], d3_in.at[i, h, dp], dec_send.at[3 + h, i], half_recv.at[2, i, h], (sect, me, to)
-                ).start()
-            d3_in[i, h, dp] = d3_out[i, h, dp]
+                from_here, to_there = d3_out[h].at[i, to], d3_in[h].at[i, dp]
+                rcopy(from_here, to_there, dec_send.at[3 + h, i], half_recv.at[2, i, h], (sect, me, to)).start()
+            d3_in[h][i, dp] = d3_out[h][i, dp]
 
         def give_back(h):
-            wait_here(d3_in.at[i, h, pl.ds(0, shards - 1)], half_recv.at[2, i, h])
-            total = d3_in[i, h, 0].astype(f32)
+            first, size = firsts[h], sizes[h]
+            wait_here(d3_in[h].at[i, pl.ds(0, shards - 1)], half_recv.at[2, i, h])
+            total = d3_in[h][i, 0].astype(f32)
             for q in range(1, shards):
-                total += d3_in[i, h, q].astype(f32)
+                total += d3_in[h][i, q].astype(f32)
             total = total.astype(bf16)
-            back = dot(give_d[0], total[:, :LANES]) + dot(give_d[1], total[:, LANES:])
-            d4_out[i, h * half : (h + 1) * half] = back.astype(bf16).reshape(half, 8, LANES)
-            for k in sect_far_first:
+            back = dot(give_d[h][0], total[:, :LANES]) + dot(give_d[h][1], total[:, LANES:])
+            d4_out[i, first : first + size] = back.astype(bf16).reshape(size, 8, LANES)
+            for k in sect_far_first + ([0] if hand_over else []):
                 place = (k - low) % experts
-                if place // half == h:
+                if first <= place < first + size:
                     to = lax.rem(me + experts - k, experts)
-                    rcopy(d4_out.at[i, place], d4_in.at[i, me], dec_send.at[5, i], ends_recv.at[i], (sect, to, dp)).start()
+                    home, slot = (other, 2) if hand_over else (sect, i)
+                    rcopy(
+                        d4_out.at[i, place], d4_in.at[slot, me], dec_send.at[5, i], ends_recv.at[slot], (home, to, dp)
+                    ).start()
 
         gather(1)
         gather(0)
+        if meanwhile is not None:
+            meanwhile()
         near_act = up_part(1)
         down_part(0, up_part(0))
         down_part(1, near_act)
         give_back(0)
         give_back(1)
-        d4_in[i, me] = d4_out[i, own_place]
+        if not hand_over:
+            d4_in[i, me] = d4_out[i, own_place]
+            mix(i, experts - 1)
+
+    def mix(i, blocks):
         lane_ids = iota((2 * dec_rows, experts * 8), 1)
-        mix = jnp.where(lane_ids == tcol_ref[i, 0], gcol_ref[i, 0], 0.0)
-        mix += jnp.where(lane_ids == tcol_ref[i, 1], gcol_ref[i, 1], 0.0)
-        high = mix.astype(bf16)
-        rest = mix - high.astype(f32)
+        weight = jnp.where(lane_ids == tcol_ref[i, 0], gcol_ref[i, 0], 0.0)
+        weight += jnp.where(lane_ids == tcol_ref[i, 1], gcol_ref[i, 1], 0.0)
+        high = weight.astype(bf16)
+        rest = weight - high.astype(f32)
         middle = rest.astype(bf16)
-        low_part = (rest - middle.astype(f32)).astype(bf16)
-        wait_here(d4_in.at[i, pl.ds(0, experts - 1)], ends_recv.at[i])
+        lowest = (rest - middle.astype(f32)).astype(bf16)
+        wait_here(d4_in.at[i, pl.ds(0, blocks)], ends_recv.at[i])
         returned = d4_in[i].reshape(experts * 8, LANES)
-        states_ref[...] += dot(high, returned) + (dot(middle, returned) + dot(low_part, returned))
-
-    def decode_sent(i):
+        states_ref[...] += dot(high, returned) + (dot(middle, returned) + dot(lowest, returned))
+
+    def decode_sent(i, blocks):
         wait_sent(d1_out.at[i, pl.ds(0, experts - 1)], dec_send.at[0, i])
         for h in range(2):
-            wait_sent(xg.at[i, h, pl.ds(0, shards - 1)], dec_send.at[1 + h, i])
-            wait_sent(d3_out.at[i, h, pl.ds(0, shards - 1)], dec_send.at[3 + h, i])
-        wait_sent(d4_out.at[i, pl.ds(0, experts - 1)], dec_send.at[5, i])
+            wait_sent(xg[h].at[i, pl.ds(0, shards - 1)], dec_send.at[1 + h, i])
+            wait_sent(d3_out[h].at[i, pl.ds(0, shards - 1)], dec_send.at[3 + h, i])
+        wait_sent(d4_out.at[i, pl.ds(0, blocks)], dec_send.at[5, i])
 
     @pl.when(sect == 0)
     def _():
@@ -252,16 +267,16 @@
         rcopy(own_v, held, l1_sem.at[0], l1_sem.at[1], (other, me, dp)).start()
         loads[3].wait()
         loads[4].wait()
+        decode_step(0, up_v, down_v)
+        rcopy(states_ref, states_ref, st_sem.at[0], st_sem.at[1], (other, me, dp)).start()
+        decode_step(1, up_v, down_v, hand_over=True)
+        wait_sent(states_ref, st_sem.at[0])
+        wait_sent(held, l1_sem.at[0])
+        decode_sent(0, experts - 1)
+        decode_sent(1, experts)
+        wait_here(fresh_up_ref, fresh_sem.at[0, 1])
         for i in range(2):
-            decode_step(i, i, up_v, down_v)
-        move = rcopy(states_ref, states_ref, st_sem.at[0], st_sem.at[1], (other, me, dp))
-        move.start()
-        move.wait_send()
-        wait_sent(held, l1_sem.at[0])
-        for i in range(2):
-            decode_sent(i)
-        wait_here(fresh_up_ref, fresh_sem.at[0, 1])
-        wait_here(fresh_down_ref, fresh_sem.at[1, 1])
+            wait_here(fresh_down_ref.at[pl.ds(i * (hidden // 2), hidden // 2)], fresh_sem.at[1 + i, 1])
         wait_here(final_ref, fin_sem.at[1])
 
     @pl.when(sect == 1)
@@ -289,6 +304,7 @@
             load.wait()
         for i in range(2):
             tables(i, i + 2)
+        tables(2, 1)
         greeted()
         wait_here(held, l1_sem.at[1])
         for j in range(2):
@@ -404,11 +420,19 @@
                 rhs = jnp.concatenate([xg4[g, q % 2, q // 2, j] for g in range(GROUPS)], axis=0)
                 grad = dot_tn(lhs, rhs) * scale
                 new[:, cols] = (old[:, cols].astype(f32) - step_size * grad).astype(bf16)
-            rcopy(new, new, fresh_sem.at[j, 0], fresh_sem.at[j, 1], (other, me, dp)).start()
+            if j == 0:
+                rcopy(new, new, fresh_sem.at[j, 0], fresh_sem.at[j, 1], (other, me, dp)).start()
 
         wait_here(states_ref, st_sem.at[1])
+        mix(2, experts)
         for i in range(2):
-            decode_step(i, i + 2, fresh_up_ref, fresh_down_ref)
+
+            def send_fresh(i=i):
+                rows = pl.ds(i * (hidden // 2), hidden // 2)
+                piece = fresh_down_ref.at[rows]
+                rcopy(piece, piece, fresh_sem.at[1 + i, 0], fresh_sem.at[1 + i, 1], (other, me, dp)).start()
+
+            decode_step(i, fresh_up_ref, fresh_down_ref, meanwhile=send_fresh)
 
         last = states_ref[...].astype(bf16)
         fin_src[...] = jnp.concatenate([last[:dec_rows], last[dec_rows:]], axis=1)
@@ -442,7 +466,7 @@
             wait_sent(final_ref.at[:, pl.ds(0, (near - 1) * part)], fin_sem.at[0])
 
         for i in range(2):
-            decode_sent(i)
+            decode_sent(i, experts - 1)
         wait_sent(out2.at[:, pl.ds(0, experts - 1)], l2_sem.at[0])
         wait_sent(out3.at[:, pl.ds(0, experts - 1)], l3_send)
         for g in range(GROUPS):
@@ -452,7 +476,8 @@
             wait_sent(xg4.at[g, core, ring, 1], l4_send.at[3, g])
             wait_sent(xg4.at[g, core], l4_send.at[4, g])
         wait_sent(fresh_up_ref, fresh_sem.at[0, 0])
-        wait_sent(fresh_down_ref, fresh_sem.at[1, 0])
+        for i in range(2):
+            wait_sent(fresh_down_ref.at[pl.ds(i * (hidden // 2), hidden // 2)], fresh_sem.at[1 + i, 0])
 
 
 def on_device(
@@ -466,7 +491,7 @@
     hidden = up_weight.shape[2]
     cap_d = 3 * dec_rows * 2 // (2 * experts)
     cap_l = 3 * lrn_rows * 2 // (2 * experts)
-    slots = experts * cap_d
+    sizes = (experts // 4, experts - experts // 4)
     group_slots = experts // GROUPS * cap_l
     half_rows = traj_inputs.shape[1]
     vmem = pl.BlockSpec(memory_space=pltpu.VMEM)
@@ -484,15 +509,13 @@
         scratch_shapes=[
             pltpu.VMEM((2, experts, 8, LANES), bf16),
             pltpu.VMEM((2, experts, 8, LANES), bf16),
-            pltpu.VMEM((2, 2, shards, slots // 2, part), bf16),
-            pltpu.VMEM((2, 2, shards, slots // 2, part), bf16),
-            pltpu.VMEM((2, 2, shards, slots // 2, part), bf16),
+            *[pltpu.VMEM((2, shards, size * cap_d, part), bf16) for _ in range(3) for size in sizes],
             pltpu.VMEM((2, experts, 8, LANES), bf16),
-            pltpu.VMEM((2, experts, 8, LANES), bf16),
+            pltpu.VMEM((3, experts, 8, LANES), bf16),
             pltpu.VMEM((2 * dec_rows, LANES), f32),
-            pltpu.VMEM((2, 2, 1, 2 * dec_rows), f32),
-            pltpu.VMEM((2, 2, 2 * dec_rows, 1), f32),
-            pltpu.VMEM((2, 2, 2 * dec_rows, 1), f32),
+            pltpu.VMEM((3, 2, 1, 2 * dec_rows), f32),
+            pltpu.VMEM((3, 2, 2 * dec_rows, 1), f32),
+            pltpu.VMEM((3, 2, 2 * dec_rows, 1), f32),
             pltpu.VMEM((2, half_rows, part), bf16),
             pltpu.VMEM((2, experts, 8, LANES), bf16),
             pltpu.VMEM((2, experts, 8, LANES), bf16),
@@ -506,18 +529,18 @@
             pltpu.VMEM((hidden, width), bf16),
             pltpu.VMEM((dec_rows, part), bf16),
             pltpu.VMEM((2, half_rows, part), bf16),
-            pltpu.VMEM((2, slots // 2, experts * 4), bf16),
-            pltpu.VMEM((2, experts * 4, slots // 2), bf16),
+            *[pltpu.VMEM((2, size * cap_d, size * 8), bf16) for size in sizes],
+            *[pltpu.VMEM((2, size * 8, size * cap_d), bf16) for size in sizes],
             pltpu.VMEM((2, group_slots, 2 * group_slots), bf16),
             dma((5,)),
             dma((6, 2)),
-            dma((2,)),
+            dma((3,)),
             dma((3, 2, 2)),
             dma((2,)),
             dma((2,)),
             dma((2,)),
             dma((2,)),
-            dma((2, 2)),
+            dma((3, 2)),
             dma,
             dma((GROUPS,)),
             dma((5, GROUPS)),

time: 155 us -> 141 us (0.910)
  Pallas kernels: 149 us -> 136 us
    pallas_call x1, Pallas kernels: 149 us -> 136 us  [on_device(): pl.pallas_call(functools.partial(kernel, experts, shards, cap_d, cap_l),...]
where the time goes in v3:
time: 141 us
  Pallas kernels  136 us (96%)
  local copies, waits for them, and re-layouts  4.52 us (3%)
    pallas_call x1, Pallas kernels, on_device(): pl.pallas_call(functools.partial(kernel, experts, shards, cap_d, cap_l),...  136 us
    unnamed x5, local copies, waits for them, and re-layouts  4.52 us

profile of v3, /device:TPU:1, one launch (start us, length us, event | category | flops | bytes accessed | tf_op | source)
XLA Modules:
  0.0 141.0 jit_solution(7993235127772264156)
XLA Ops:
  0.6 135.8 %shard_map.139 = (bf16[32,1024]{1,0:T(8,128)(2,1)}, bf16[192,2048]{1,0:T(8,128)(2,1)}, bf16[192,2048]{1,0:T(8,128)(2,1)}) custom-call(bf16[32,2048]{1,0:T(8,128)(2,1)} %rows_ref.1, f32[16,128]{1,0:T(8,128)} %bitcast.18, s32[4,2,32]{2,1,0:T(2,128)} %bitcast.19, f32[4,2,32]{2,1,0:T(2,128)} %bitcast.20, bf16[192,2048]{1,0:T(8,128)(2,1)} %bitcast.12, ...), custom_call_target="tpu_custom_call" | custom-call | tf_op jit(solution)/shard_map/pallas_call | solution.py:500
  136.4 1.5 %copy.18 = bf16[32,1024]{1,0:T(8,128)(2,1)} copy(bf16[32,1024]{1,0:T(8,128)(2,1)} %get-tuple-element.12) | data formatting | bytes 131072
  137.9 0.0 copy-start
  137.9 2.2 %copy.19 = bf16[1,1,192,2048]{3,2,1,0:T(8,128)(2,1)} copy(bf16[1,1,192,2048]{3,2,1,0:T(8,128)(2,1)} %bitcast.15) | data formatting | bytes 1572864
  140.1 0.0 copy-done
  140.1 0.9 copy.20
Async XLA Ops:
  137.9 2.2 %copy-start = (bf16[192,2048]{1,0:T(8,128)(2,1)S(1)}, bf16[192,2048]{1,0:T(8,128)(2,1)}, u32[]{:S(2)}) copy-start(bf16[192,2048]{1,0:T(8,128)(2,1)} %get-tuple-element.8) | copy-start | bytes 2359300

commit v4 on v3

--- a/solution.py
+++ b/solution.py
@@ -90,7 +90,7 @@
     per = experts // GROUPS
     group_slots = per * cap_l
     col0 = pl.multiple_of(dp * part, part)
-    sizes = (experts // 4, experts - experts // 4)
+    sizes = (experts * 1 // 2, experts - experts * 1 // 2)
     firsts = (0, sizes[0])
     low = (experts - sizes[0] + 1) // 2
     xg, d3_out, d3_in = (xg_far, xg_near), (d3_out_far, d3_out_near), (d3_in_far, d3_in_near)
@@ -226,11 +226,10 @@
         gather(0)
         if meanwhile is not None:
             meanwhile()
-        near_act = up_part(1)
+        down_part(1, up_part(1))
         down_part(0, up_part(0))
-        down_part(1, near_act)
+        give_back(1)
         give_back(0)
-        give_back(1)
         if not hand_over:
             d4_in[i, me] = d4_out[i, own_place]
             mix(i, experts - 1)
@@ -491,12 +490,13 @@
     hidden = up_weight.shape[2]
     cap_d = 3 * dec_rows * 2 // (2 * experts)
     cap_l = 3 * lrn_rows * 2 // (2 * experts)
-    sizes = (experts // 4, experts - experts // 4)
+    sizes = (experts * 1 // 2, experts - experts * 1 // 2)
     group_slots = experts // GROUPS * cap_l
     half_rows = traj_inputs.shape[1]
     vmem = pl.BlockSpec(memory_space=pltpu.VMEM)
     hbm = pl.BlockSpec(memory_space=pltpu.HBM)
     dma = pltpu.SemaphoreType.DMA
+    keep = functools.partial(pltpu.with_memory_space_constraint, memory_space=pltpu.HBM)
     final, fresh_up, fresh_down = pl.pallas_call(
         functools.partial(kernel, experts, shards, cap_d, cap_l),
         out_shape=(
@@ -547,12 +547,12 @@
             dma((5, GROUPS)),
         ],
         compiler_params=pltpu.CompilerParams(
-            collective_id=0, has_side_effects=True, vmem_limit_bytes=56 * 2**20
+            collective_id=0, has_side_effects=True, vmem_limit_bytes=40 * 2**20
         ),
     )(
-        decode_states, norm_gain.reshape(width // LANES, LANES),
+        keep(decode_states), norm_gain.reshape(width // LANES, LANES),
         decode_routes.transpose(0, 2, 1), decode_gates.transpose(0, 2, 1),
-        up_weight[0, 0], down_weight[0, 0], traj_inputs[0], traj_cotangents[0], traj_lengths[0], packing,
+        keep(up_weight[0, 0]), keep(down_weight[0, 0]), keep(traj_inputs[0]), keep(traj_cotangents[0]), traj_lengths[0], packing,
         learner_routes.T, learner_gates.T,
     )
     return final, fresh_up[None, None], fresh_down[None, None]

time: 141 us -> 137 us (0.972)
  Pallas kernels: 136 us -> 132 us
    pallas_call x1, Pallas kernels: 136 us -> 132 us  [on_device(): pl.pallas_call(functools.partial(kernel, experts, shards, cap_d, cap_l),...]
    unnamed x5 -> x17, local copies, waits for them, and re-layouts: 4.52 us -> 3.78 us
where the time goes in v4:
time: 137 us; the launch traced here: 136 us
  Pallas kernels  132 us (96%)
  local copies, waits for them, and re-layouts  3.78 us (3%)
    pallas_call x1, Pallas kernels, on_device(): pl.pallas_call(functools.partial(kernel, experts, shards, cap_d, cap_l),...  132 us
    unnamed x17, local copies, waits for them, and re-layouts  3.78 us

profile of v4, /device:TPU:1, one launch (start us, length us, event | category | flops | bytes accessed | tf_op | source)
XLA Modules:
  0.0 136.4 jit_solution(9633954340939607547)
XLA Ops:
  0.6 0.0 copy-start.4
  0.6 0.0 copy-start.6
  0.7 0.0 copy-start.2
  0.7 0.0 copy-start
  0.7 0.0 copy-start.1
  0.7 0.0 copy-start.3
  0.7 0.6 copy-done.4
  1.3 0.0 copy-done.6
  1.3 0.0 copy-done.2
  1.4 0.0 copy-done
  1.4 0.0 copy-done.1
  1.4 0.0 copy-done.3
  1.4 0.0 copy-start.5
  1.4 0.7 copy-done.5
  2.1 131.9 %shard_map.139 = (bf16[32,1024]{1,0:T(8,128)(2,1)S(1)}, bf16[192,2048]{1,0:T(8,128)(2,1)S(1)}, bf16[192,2048]{1,0:T(8,128)(2,1)S(1)}) custom-call(bf16[32,2048]{1,0:T(8,128)(2,1)} %rows_ref.1, f32[16,128]{1,0:T(8,128)S(1)} %bitcast.14, s32[4,2,32]{2,1,0:T(2,128)S(1)} %bitcast.15, f32[4,2,32]{2,1,0:T(2,128)S(1)} %bitcast.16, bf16[192,2048]{1,0:T(8,128)(2,1)} %bitcast.20, ...), custom_call_target="tpu_custom_call" | custom-call | tf_op jit(solution)/shard_map/pallas_call | solution.py:500
  134.0 0.6 copy.18
  134.6 0.9 copy.19
  135.5 0.9 copy.20
Async XLA Ops:
  0.6 0.7 copy-start.4
  0.6 0.7 copy-start.6
  0.7 0.7 copy-start.2
  0.7 0.7 copy-start
  0.7 0.7 copy-start.1
  0.7 0.7 copy-start.3
  1.4 0.7 copy-start.5

commit v5 on v3

--- a/solution.py
+++ b/solution.py
@@ -73,10 +73,10 @@
     rows_ref, gain_ref, routes_ref, gates_ref, up_ref, down_ref, in_ref, cot_ref, len_ref, pack_ref,
     lroutes_ref, lgates_ref,
     final_ref, fresh_up_ref, fresh_down_ref,
-    d1_out, d1_in, xg_far, xg_near, d3_out_far, d3_out_near, d3_in_far, d3_in_near, d4_out, d4_in, states_ref, trow_ref, tcol_ref, gcol_ref,
+    d1_out, d1_in, xg_far, xg_near, d3_out_far, d3_out_near, d3_in_far, d3_in_near, pair_in, d3_sum, d4_out, d4_in, states_ref, last_ref, trow_ref, tcol_ref, gcol_ref,
     held, out2, recv2, out3, recv3, xg4, act_ref, pre_ref, fin_src,
     up_v, down_v, rows_v, own_v, take_far, take_near, give_far, give_near, take_l,
-    load_sem, dec_send, ends_recv, half_recv, l1_sem, l2_sem, st_sem, fin_sem, fresh_sem, l3_send, l3_recv, l4_send, l4_recv,
+    load_sem, dec_send, ends_recv, half_recv, pair_recv, l1_sem, l2_sem, st_sem, last_sem, fin_sem, fresh_sem, l3_send, l3_recv, l4_send, l4_recv,
 ):
     sect, me, dp = lax.axis_index("sect"), lax.axis_index("exp"), lax.axis_index("dp")
     ring, core = lax.div(dp, 2), lax.rem(dp, 2)
@@ -90,10 +90,9 @@
     per = experts // GROUPS
     group_slots = per * cap_l
     col0 = pl.multiple_of(dp * part, part)
-    sizes = (experts // 4, experts - experts // 4)
+    sizes = (experts * 3 // 8, experts - experts * 3 // 8)
     firsts = (0, sizes[0])
     low = (experts - sizes[0] + 1) // 2
-    xg, d3_out, d3_in = (xg_far, xg_near), (d3_out_far, d3_out_near), (d3_in_far, d3_in_near)
     take_d, give_d = (take_far, take_near), (give_far, give_near)
     sect_far_first = far_first(experts)
     loads = [
@@ -108,6 +107,13 @@
         return pltpu.make_async_remote_copy(
             src_ref=src, dst_ref=dst, send_sem=send, recv_sem=recv, device_id=device, device_id_type=MESH
         )
+
+    nx = shards // 2
+    near_dp = shards // 2
+    sibling = (sect, me, ring * 2 + 1 - core)
+
+    def at_ring(position):
+        return (sect, me, position * 2 + core)
 
     def wait_sent(ref, sem):
         rcopy(ref, ref, sem, sem, (sect, me, dp)).wait_send()
@@ -152,7 +158,7 @@
             gate = to_col(gates_ref[t, k : k + 1, :])
             gcol_ref[i, k] = jnp.concatenate([gate, gate], axis=0)
 
-    def decode_step(i, up, down, meanwhile=None, hand_over=False):
+    def decode_step(i, up, down, meanwhile=None, hand_over=False, split=False):
         gain0, gain1 = gain_ref[pl.ds(2 * dp, 1), :], gain_ref[pl.ds(2 * dp + 1, 1), :]
         gains = jnp.concatenate(
             [jnp.broadcast_to(gain0, (dec_rows, LANES)), jnp.broadcast_to(gain1, (dec_rows, LANES))], axis=0
@@ -175,18 +181,33 @@
             wait_here(d1_in.at[i, pl.ds(first, size - h)], half_recv.at[0, i, h])
             arrived = d1_in[i, first : first + size].reshape(size * 8, LANES)
             block = [dot(take_d[h][c], arrived).astype(bf16) for c in range(2)]
-            xg[h][i, dp] = jnp.concatenate(block, axis=1)
-            mine = xg[h].at[i, dp]
-            for q in far_first(shards):
-                to = lax.rem(dp + q, shards)
-                rcopy(mine, mine, dec_send.at[1 + h, i], half_recv.at[1, i, h], (sect, me, to)).start()
+            if h == 0:
+                xg_far[i, dp] = jnp.concatenate(block, axis=1)
+                mine = xg_far.at[i, dp]
+                for q in far_first(shards):
+                    to = lax.rem(dp + q, shards)
+                    rcopy(mine, mine, dec_send.at[1, i], half_recv.at[1, i, 0], (sect, me, to)).start()
+            else:
+                xg_near[i, core, ring] = jnp.concatenate(block, axis=1)
+                mine = xg_near.at[i, core, ring]
+                for k in far_first(nx):
+                    to = at_ring(lax.rem(ring + k, nx))
+                    rcopy(mine, mine, dec_send.at[2, i], half_recv.at[1, i, 1], to).start()
+
+        def share_near():
+            wait_here(xg_near.at[i, core, pl.ds(0, nx - 1)], half_recv.at[1, i, 1])
+            mine = xg_near.at[i, core]
+            rcopy(mine, mine, dec_send.at[6, i], pair_recv.at[0, i], sibling).start()
 
         def up_part(h):
-            wait_here(xg[h].at[i, pl.ds(0, shards - 1)], half_recv.at[1, i, h])
+            if h == 0:
+                wait_here(xg_far.at[i, pl.ds(0, shards - 1)], half_recv.at[1, i, 0])
+            else:
+                wait_here(xg_near.at[i, 1 - core], pair_recv.at[0, i])
             before_act = jnp.zeros((sizes[h] * cap_d, hidden), f32)
             squares = jnp.zeros((sizes[h] * cap_d, part), f32)
             for q in range(shards):
-                piece = xg[h][i, q]
+                piece = xg_far[i, q] if h == 0 else xg_near[i, q % 2, q // 2]
                 before_act += dot_nt(piece, up[:, q * part : (q + 1) * part])
                 gain = jnp.concatenate([gain_ref[2 * q : 2 * q + 1], gain_ref[2 * q + 1 : 2 * q + 2]], axis=1)
                 wide = piece.astype(f32) * (1.0 / gain)
@@ -197,19 +218,37 @@
 
         def down_part(h, act):
             for q in range(shards):
-                d3_out[h][i, q] = (dot(act, down[:, q * part : (q + 1) * part]) * hidden_scale).astype(bf16)
-            for q in far_first(shards):
-                to = lax.rem(dp + q, shards)
-                from_here, to_there = d3_out[h].at[i, to], d3_in[h].at[i, dp]
-                rcopy(from_here, to_there, dec_send.at[3 + h, i], half_recv.at[2, i, h], (sect, me, to)).start()
-            d3_in[h][i, dp] = d3_out[h][i, dp]
+                piece = (dot(act, down[:, q * part : (q + 1) * part]) * hidden_scale).astype(bf16)
+                if h == 0:
+                    d3_out_far[i, q] = piece
+                else:
+                    d3_out_near[i, q % 2, q // 2] = piece
+            if h == 0:
+                for q in far_first(shards):
+                    to = lax.rem(dp + q, shards)
+                    from_here, to_there = d3_out_far.at[i, to], d3_in_far.at[i, dp]
+                    rcopy(from_here, to_there, dec_send.at[3, i], half_recv.at[2, i, 0], (sect, me, to)).start()
+                d3_in_far[i, dp] = d3_out_far[i, dp]
+            else:
+                theirs = d3_out_near.at[i, 1 - core]
+                rcopy(theirs, pair_in.at[i], dec_send.at[7, i], pair_recv.at[1, i], sibling).start()
+
+        def scatter_near():
+            wait_here(pair_in.at[i], pair_recv.at[1, i])
+            d3_sum[i] = (d3_out_near[i, core].astype(f32) + pair_in[i].astype(f32)).astype(bf16)
+            for k in far_first(nx):
+                to = lax.rem(ring + k, nx)
+                from_here, to_there = d3_sum.at[i, to], d3_in_near.at[i, ring]
+                rcopy(from_here, to_there, dec_send.at[4, i], half_recv.at[2, i, 1], at_ring(to)).start()
+            d3_in_near[i, ring] = d3_sum[i, ring]
 
         def give_back(h):
             first, size = firsts[h], sizes[h]
-            wait_here(d3_in[h].at[i, pl.ds(0, shards - 1)], half_recv.at[2, i, h])
-            total = d3_in[h][i, 0].astype(f32)
-            for q in range(1, shards):
-                total += d3_in[h][i, q].astype(f32)
+            d3_in, count = (d3_in_far, shards) if h == 0 else (d3_in_near, nx)
+            wait_here(d3_in.at[i, pl.ds(0, count - 1)], half_recv.at[2, i, h])
+            total = d3_in[i, 0].astype(f32)
+            for q in range(1, count):
+                total += d3_in[i, q].astype(f32)
             total = total.astype(bf16)
             back = dot(give_d[h][0], total[:, :LANES]) + dot(give_d[h][1], total[:, LANES:])
             d4_out[i, first : first + size] = back.astype(bf16).reshape(size, 8, LANES)
@@ -218,24 +257,39 @@
                 if first <= place < first + size:
                     to = lax.rem(me + experts - k, experts)
                     home, slot = (other, 2) if hand_over else (sect, i)
+                    if split:
+                        home, slot = jnp.where(dp < near_dp, other, sect), jnp.where(dp < near_dp, 2, i)
                     rcopy(
                         d4_out.at[i, place], d4_in.at[slot, me], dec_send.at[5, i], ends_recv.at[slot], (home, to, dp)
                     ).start()
 
         gather(1)
         gather(0)
+        share_near()
         if meanwhile is not None:
             meanwhile()
         near_act = up_part(1)
         down_part(0, up_part(0))
         down_part(1, near_act)
+        scatter_near()
         give_back(0)
         give_back(1)
-        if not hand_over:
+        if split:
+            @pl.when(dp < near_dp)
+            def _():
+                rcopy(
+                    d4_out.at[i, own_place], d4_in.at[2, me], dec_send.at[5, i], ends_recv.at[2], (other, me, dp)
+                ).start()
+
+            @pl.when(dp >= near_dp)
+            def _():
+                d4_in[i, me] = d4_out[i, own_place]
+                mix(i, experts - 1, states_ref)
+        elif not hand_over:
             d4_in[i, me] = d4_out[i, own_place]
-            mix(i, experts - 1)
-
-    def mix(i, blocks):
+            mix(i, experts - 1, states_ref)
+
+    def mix(i, blocks, onto):
         lane_ids = iota((2 * dec_rows, experts * 8), 1)
         weight = jnp.where(lane_ids == tcol_ref[i, 0], gcol_ref[i, 0], 0.0)
         weight += jnp.where(lane_ids == tcol_ref[i, 1], gcol_ref[i, 1], 0.0)
@@ -245,13 +299,29 @@
         lowest = (rest - middle.astype(f32)).astype(bf16)
         wait_here(d4_in.at[i, pl.ds(0, blocks)], ends_recv.at[i])
         returned = d4_in[i].reshape(experts * 8, LANES)
-        states_ref[...] += dot(high, returned) + (dot(middle, returned) + dot(lowest, returned))
+        onto[...] += dot(high, returned) + (dot(middle, returned) + dot(lowest, returned))
+
+    out_cols = pl.ds(pl.multiple_of(lax.rem(dp, near_dp) * part, part), part)
+
+    def finish(from_ref):
+        last = from_ref[...].astype(bf16)
+        fin_src[...] = jnp.concatenate([last[:dec_rows], last[dec_rows:]], axis=1)
+        for q in far_first(shards):
+            to = lax.rem(dp + q, shards)
+            rcopy(fin_src, final_ref.at[:, out_cols], fin_sem.at[0], fin_sem.at[1], (sect, me, to)).start()
+        final_ref[:, out_cols] = fin_src[...]
+        wait_here(final_ref.at[:, pl.ds(0, (near_dp - 1) * part)], fin_sem.at[1])
+        wait_sent(final_ref, fin_sem.at[0])
+        wait_sent(final_ref.at[:, pl.ds(0, (near_dp - 1) * part)], fin_sem.at[0])
 
     def decode_sent(i, blocks):
         wait_sent(d1_out.at[i, pl.ds(0, experts - 1)], dec_send.at[0, i])
-        for h in range(2):
-            wait_sent(xg[h].at[i, pl.ds(0, shards - 1)], dec_send.at[1 + h, i])
-            wait_sent(d3_out[h].at[i, pl.ds(0, shards - 1)], dec_send.at[3 + h, i])
+        wait_sent(xg_far.at[i, pl.ds(0, shards - 1)], dec_send.at[1, i])
+        wait_sent(xg_near.at[i, core, pl.ds(0, nx - 1)], dec_send.at[2, i])
+        wait_sent(d3_out_far.at[i, pl.ds(0, shards - 1)], dec_send.at[3, i])
+        wait_sent(d3_sum.at[i, pl.ds(0, nx - 1)], dec_send.at[4, i])
+        wait_sent(xg_near.at[i, core], dec_send.at[6, i])
+        wait_sent(d3_out_near.at[i, core], dec_send.at[7, i])
         wait_sent(d4_out.at[i, pl.ds(0, blocks)], dec_send.at[5, i])
 
     @pl.when(sect == 0)
@@ -270,14 +340,25 @@
         decode_step(0, up_v, down_v)
         rcopy(states_ref, states_ref, st_sem.at[0], st_sem.at[1], (other, me, dp)).start()
         decode_step(1, up_v, down_v, hand_over=True)
+        tables(2, 3)
         wait_sent(states_ref, st_sem.at[0])
         wait_sent(held, l1_sem.at[0])
         decode_sent(0, experts - 1)
         decode_sent(1, experts)
+
+        @pl.when(dp < near_dp)
+        def _():
+            wait_here(last_ref, last_sem.at[1])
+            mix(2, experts, last_ref)
+            finish(last_ref)
+
+        @pl.when(dp >= near_dp)
+        def _():
+            wait_here(final_ref, fin_sem.at[1])
+
         wait_here(fresh_up_ref, fresh_sem.at[0, 1])
         for i in range(2):
             wait_here(fresh_down_ref.at[pl.ds(i * (hidden // 2), hidden // 2)], fresh_sem.at[1 + i, 1])
-        wait_here(final_ref, fin_sem.at[1])
 
     @pl.when(sect == 1)
     def _():
@@ -356,11 +437,7 @@
         recv3[0, 0] = out3[0, me]
         recv3[1, 0] = out3[1, me]
 
-        nx = shards // 2
         right, left = lax.rem(ring + 1, nx), lax.rem(ring + nx - 1, nx)
-
-        def at_ring(position):
-            return (sect, me, position * 2 + core)
 
         def spread(g):
             first_in = 1 if g == 0 else 0
@@ -424,7 +501,7 @@
                 rcopy(new, new, fresh_sem.at[j, 0], fresh_sem.at[j, 1], (other, me, dp)).start()
 
         wait_here(states_ref, st_sem.at[1])
-        mix(2, experts)
+        mix(2, experts, states_ref)
         for i in range(2):
 
             def send_fresh(i=i):
@@ -432,41 +509,26 @@
                 piece = fresh_down_ref.at[rows]
                 rcopy(piece, piece, fresh_sem.at[1 + i, 0], fresh_sem.at[1 + i, 1], (other, me, dp)).start()
 
-            decode_step(i, fresh_up_ref, fresh_down_ref, meanwhile=send_fresh)
-
-        last = states_ref[...].astype(bf16)
-        fin_src[...] = jnp.concatenate([last[:dec_rows], last[dec_rows:]], axis=1)
-        near = shards // 2
-        out_cols = pl.ds(pl.multiple_of(lax.rem(dp, near) * part, part), part)
-
-        @pl.when(dp < near)
+            decode_step(i, fresh_up_ref, fresh_down_ref, meanwhile=send_fresh, split=i == 1)
+            if i == 0:
+
+                @pl.when(dp < near_dp)
+                def _():
+                    rcopy(states_ref, last_ref, last_sem.at[0], last_sem.at[1], (other, me, dp)).start()
+
+        decode_sent(0, experts - 1)
+
+        @pl.when(dp < near_dp)
         def _():
-            def send_far(q, carry):
-                to = lax.rem(dp + q, shards)
-                rcopy(fin_src, final_ref.at[:, out_cols], fin_sem.at[0], fin_sem.at[1], (other, me, to)).start()
-                return carry
-
-            lax.fori_loop(0, shards, send_far, 0)
             wait_here(final_ref, fin_sem.at[1])
-            for _ in range(2):
-                wait_sent(final_ref, fin_sem.at[0])
-
-        @pl.when(dp >= near)
+            wait_sent(states_ref, last_sem.at[0])
+            decode_sent(1, experts)
+
+        @pl.when(dp >= near_dp)
         def _():
-            final_ref[:, out_cols] = fin_src[...]
-
-            def send_near(q, carry):
-                to = lax.rem(dp + q, shards)
-                rcopy(fin_src, final_ref.at[:, out_cols], fin_sem.at[0], fin_sem.at[1], (sect, me, to)).start()
-                return carry
-
-            lax.fori_loop(1, shards, send_near, 0)
-            wait_here(final_ref.at[:, pl.ds(0, (near - 1) * part)], fin_sem.at[1])
-            wait_sent(final_ref, fin_sem.at[0])
-            wait_sent(final_ref.at[:, pl.ds(0, (near - 1) * part)], fin_sem.at[0])
-
-        for i in range(2):
-            decode_sent(i, experts - 1)
+            finish(states_ref)
+            decode_sent(1, experts - 1)
+
         wait_sent(out2.at[:, pl.ds(0, experts - 1)], l2_sem.at[0])
         wait_sent(out3.at[:, pl.ds(0, experts - 1)], l3_send)
         for g in range(GROUPS):
@@ -491,12 +553,17 @@
     hidden = up_weight.shape[2]
     cap_d = 3 * dec_rows * 2 // (2 * experts)
     cap_l = 3 * lrn_rows * 2 // (2 * experts)
-    sizes = (experts // 4, experts - experts // 4)
+    sizes = (experts * 3 // 8, experts - experts * 3 // 8)
+    pairs = (2, shards // 2)
+    far, near = ((shards,), sizes[0]), (pairs, sizes[1])
+    chips = (pairs[1:], sizes[1])
+    buffers = (far, near, far, near, far, chips, chips, chips)
     group_slots = experts // GROUPS * cap_l
     half_rows = traj_inputs.shape[1]
     vmem = pl.BlockSpec(memory_space=pltpu.VMEM)
     hbm = pl.BlockSpec(memory_space=pltpu.HBM)
     dma = pltpu.SemaphoreType.DMA
+    keep = functools.partial(pltpu.with_memory_space_constraint, memory_space=pltpu.HBM)
     final, fresh_up, fresh_down = pl.pallas_call(
         functools.partial(kernel, experts, shards, cap_d, cap_l),
         out_shape=(
@@ -509,9 +576,10 @@
         scratch_shapes=[
             pltpu.VMEM((2, experts, 8, LANES), bf16),
             pltpu.VMEM((2, experts, 8, LANES), bf16),
-            *[pltpu.VMEM((2, shards, size * cap_d, part), bf16) for _ in range(3) for size in sizes],
+            *[pltpu.VMEM((2, *lead, size * cap_d, part), bf16) for lead, size in buffers],
             pltpu.VMEM((2, experts, 8, LANES), bf16),
             pltpu.VMEM((3, experts, 8, LANES), bf16),
+            pltpu.VMEM((2 * dec_rows, LANES), f32),
             pltpu.VMEM((2 * dec_rows, LANES), f32),
             pltpu.VMEM((3, 2, 1, 2 * dec_rows), f32),
             pltpu.VMEM((3, 2, 2 * dec_rows, 1), f32),
@@ -533,9 +601,11 @@
             *[pltpu.VMEM((2, size * 8, size * cap_d), bf16) for size in sizes],
             pltpu.VMEM((2, group_slots, 2 * group_slots), bf16),
             dma((5,)),
-            dma((6, 2)),
+            dma((8, 2)),
             dma((3,)),
             dma((3, 2, 2)),
+            dma((2, 2)),
+            dma((2,)),
             dma((2,)),
             dma((2,)),
             dma((2,)),
@@ -547,13 +617,13 @@
             dma((5, GROUPS)),
         ],
         compiler_params=pltpu.CompilerParams(
-            collective_id=0, has_side_effects=True, vmem_limit_bytes=56 * 2**20
+            collective_id=0, has_side_effects=True, vmem_limit_bytes=40 * 2**20
         ),
     )(
-        decode_states, norm_gain.reshape(width // LANES, LANES),
-        decode_routes.transpose(0, 2, 1), decode_gates.transpose(0, 2, 1),
-        up_weight[0, 0], down_weight[0, 0], traj_inputs[0], traj_cotangents[0], traj_lengths[0], packing,
-        learner_routes.T, learner_gates.T,
+        keep(decode_states), keep(norm_gain.reshape(width // LANES, LANES)),
+        keep(decode_routes.transpose(0, 2, 1)), keep(decode_gates.transpose(0, 2, 1)),
+        keep(up_weight[0, 0]), keep(down_weight[0, 0]), keep(traj_inputs[0]), keep(traj_cotangents[0]), keep(traj_lengths[0]), keep(packing),
+        keep(learner_routes.T), keep(learner_gates.T),
     )
     return final, fresh_up[None, None], fresh_down[None, None]
 

time: 141 us -> 133 us (0.943)
  Pallas kernels: 136 us -> 130 us
  local copies, waits for them, and re-layouts: 4.52 us -> 2.39 us
    pallas_call x1, Pallas kernels: 136 us -> 130 us  [on_device(): pl.pallas_call(functools.partial(kernel, experts, shards, cap_d, cap_l),...]
    unnamed x5 -> x3, local copies, waits for them, and re-layouts: 4.52 us -> 2.39 us
where the time goes in v5:
time: 133 us
  Pallas kernels  130 us (98%)
  local copies, waits for them, and re-layouts  2.39 us (2%)
    pallas_call x1, Pallas kernels, on_device(): pl.pallas_call(functools.partial(kernel, experts, shards, cap_d, cap_l),...  130 us

profile of v5, /device:TPU:1, one launch (start us, length us, event | category | flops | bytes accessed | tf_op | source)
XLA Modules:
  0.0 133.2 jit_solution(14139827762613699573)
XLA Ops:
  0.6 130.1 %shard_map.139 = (bf16[32,1024]{1,0:T(8,128)(2,1)S(1)}, bf16[192,2048]{1,0:T(8,128)(2,1)S(1)}, bf16[192,2048]{1,0:T(8,128)(2,1)S(1)}) custom-call(bf16[32,2048]{1,0:T(8,128)(2,1)} %rows_ref.1, f32[16,128]{1,0:T(8,128)} %bitcast.18, s32[4,2,32]{2,1,0:T(2,128)} %bitcast.19, f32[4,2,32]{2,1,0:T(2,128)} %bitcast.20, bf16[192,2048]{1,0:T(8,128)(2,1)} %bitcast.14, ...), custom_call_target="tpu_custom_call" | custom-call | tf_op jit(solution)/shard_map/pallas_call | solution.py:567
  130.8 0.6 copy.18
  131.4 0.9 copy.19
  132.3 0.9 copy.20

commit v6 on v5

--- a/solution.py
+++ b/solution.py
@@ -124,9 +124,8 @@
     barrier = pltpu.get_barrier_semaphore()
 
     for k in sect_far_first:
-        pl.semaphore_signal(barrier, inc=1, device_id=(sect, lax.rem(me + k, experts), dp), device_id_type=MESH)
-    for k in sect_far_first:
-        pl.semaphore_signal(barrier, inc=1, device_id=(other, lax.rem(me + k, experts), dp), device_id_type=MESH)
+        for home in (other, sect):
+            pl.semaphore_signal(barrier, inc=1, device_id=(home, lax.rem(me + k, experts), dp), device_id_type=MESH)
     for q in range(1, shards):
         pl.semaphore_signal(barrier, inc=1, device_id=(sect, me, lax.rem(dp + q, shards)), device_id_type=MESH)
     for q in range(shards):
@@ -158,7 +157,7 @@
             gate = to_col(gates_ref[t, k : k + 1, :])
             gcol_ref[i, k] = jnp.concatenate([gate, gate], axis=0)
 
-    def decode_step(i, up, down, meanwhile=None, hand_over=False, split=False):
+    def prepare(i):
         gain0, gain1 = gain_ref[pl.ds(2 * dp, 1), :], gain_ref[pl.ds(2 * dp + 1, 1), :]
         gains = jnp.concatenate(
             [jnp.broadcast_to(gain0, (dec_rows, LANES)), jnp.broadcast_to(gain1, (dec_rows, LANES))], axis=0
@@ -168,6 +167,8 @@
         pick = (row_ids == trow_ref[i, 0]) | (row_ids == trow_ref[i, 1])
         pick = jnp.where(pick, 1.0, 0.0).astype(bf16)
         d1_out[i] = dot(pick, y).astype(bf16).reshape(experts, 8, LANES)
+
+    def decode_step(i, up, down, meanwhile=None, hand_over=False, split=False):
         for k in sect_far_first:
             place = (k - low) % experts
             to = lax.rem(me + k, experts)
@@ -331,13 +332,13 @@
         loads[0].wait()
         rows = rows_v[...].astype(f32)
         states_ref[...] = jnp.concatenate([rows[:, :LANES], rows[:, LANES:]], axis=0)
-        loads[1].wait()
-        loads[2].wait()
+        prepare(0)
+        for load in loads[1:]:
+            load.wait()
         greeted()
         rcopy(own_v, held, l1_sem.at[0], l1_sem.at[1], (other, me, dp)).start()
-        loads[3].wait()
-        loads[4].wait()
         decode_step(0, up_v, down_v)
+        prepare(1)
         rcopy(states_ref, states_ref, st_sem.at[0], st_sem.at[1], (other, me, dp)).start()
         decode_step(1, up_v, down_v, hand_over=True)
         tables(2, 3)
@@ -509,6 +510,7 @@
                 piece = fresh_down_ref.at[rows]
                 rcopy(piece, piece, fresh_sem.at[1 + i, 0], fresh_sem.at[1 + i, 1], (other, me, dp)).start()
 
+            prepare(i)
             decode_step(i, fresh_up_ref, fresh_down_ref, meanwhile=send_fresh, split=i == 1)
             if i == 0:
 

time: 133 us -> 133 us (level)
  no operation moved by 1% of the time
where the time goes in v6:
time: 133 us
  Pallas kernels  130 us (98%)
  local copies, waits for them, and re-layouts  2.39 us (2%)
    pallas_call x1, Pallas kernels, on_device(): pl.pallas_call(functools.partial(kernel, experts, shards, cap_d, cap_l),...  130 us

profile of v6, /device:TPU:1, one launch (start us, length us, event | category | flops | bytes accessed | tf_op | source)
XLA Modules:
  0.0 132.9 jit_solution(10280199438006796898)
XLA Ops:
  0.6 129.9 %shard_map.139 = (bf16[32,1024]{1,0:T(8,128)(2,1)S(1)}, bf16[192,2048]{1,0:T(8,128)(2,1)S(1)}, bf16[192,2048]{1,0:T(8,128)(2,1)S(1)}) custom-call(bf16[32,2048]{1,0:T(8,128)(2,1)} %rows_ref.1, f32[16,128]{1,0:T(8,128)} %bitcast.18, s32[4,2,32]{2,1,0:T(2,128)} %bitcast.19, f32[4,2,32]{2,1,0:T(2,128)} %bitcast.20, bf16[192,2048]{1,0:T(8,128)(2,1)} %bitcast.14, ...), custom_call_target="tpu_custom_call" | custom-call | tf_op jit(solution)/shard_map/pallas_call | solution.py:569
  130.5 0.6 copy.18
  131.1 0.9 copy.19
  132.0 0.9 copy.20
